TPU v7x, 256 devices: a whole 4x4x8 slice. The times are simulated.
256 devices in a mesh: dp: 4 (over y), seq: 64 (over x, z, core).
Axes of the slice: x: 4, y: 4, z: 8, core: 2. Of those that a mesh axis runs over, the one named last changes fastest.
Arguments:
- values: bfloat16 [8, 49152, 1024], P('dp', 'seq'), may hold values from -6 to 6
- gates: bfloat16 [8, 49152, 1024], P('dp', 'seq'), may hold values from 0.25 to 4
- grad_out: bfloat16 [8, 49152, 1024], P('dp', 'seq'), may hold values from -4 to 4
- first_blocks: bfloat16 [192, 256, 256], P('seq'), may hold values from -0.375 to 0.375
- second_blocks: bfloat16 [256, 192, 192], P('seq'), may hold values from -0.4375 to 0.4375
Outputs:
- grad_values: bfloat16 [8, 49152, 1024], P('dp', 'seq')
- grad_first: float32 [192, 256, 256], P('seq')
- grad_second: float32 [256, 192, 192], P('seq')
All inputs are finite; a program needn't handle non-finite values.
Results may differ from a plain program's by a relative error of at most 0.0058.
Values may be sent and summed in bfloat16 or wider, within the bound.
No kernel may reach another device: no remote copies, remote signals or barrier semaphores. Data moves between devices by JAX's collectives and lax.ppermute only.
A program may use at most 128 MiB of HBM per device.

v0:
```python
import jax
import jax.numpy as jnp
from jax import lax
from jax.sharding import PartitionSpec as P


def shards(values, gates, grad_out, first_blocks, second_blocks):
    count, rows, width = values.shape
    local_blocks, order, _ = first_blocks.shape
    inputs = values.reshape(count, local_blocks, order, width)
    mixed = jnp.einsum(
        "nabd,abc->nacd", inputs, first_blocks, preferred_element_type=jnp.float32
    ).astype(jnp.bfloat16)
    scaled = (grad_out.astype(jnp.float32) * gates.astype(jnp.float32)).astype(jnp.bfloat16)
    scaled = scaled.reshape(count, local_blocks, order, width)
    mixed_cols = lax.all_to_all(mixed, "seq", split_axis=2, concat_axis=1, tiled=True)
    scaled_cols = lax.all_to_all(scaled, "seq", split_axis=2, concat_axis=1, tiled=True)
    inner = lax.all_to_all(
        jnp.einsum(
            "cae,necd->nacd", second_blocks, scaled_cols, preferred_element_type=jnp.float32
        ).astype(jnp.bfloat16),
        "seq",
        split_axis=1,
        concat_axis=2,
        tiled=True,
    )
    grad_second = jnp.einsum(
        "nacd,necd->cae", mixed_cols, scaled_cols, preferred_element_type=jnp.float32
    )
    grad_first = jnp.einsum("nabd,nacd->abc", inputs, inner, preferred_element_type=jnp.float32)
    grad_values = jnp.einsum(
        "abc,nacd->nabd", first_blocks, inner, preferred_element_type=jnp.float32
    ).astype(jnp.bfloat16)
    grad_first, grad_second = lax.psum((grad_first, grad_second), "dp")
    return (grad_values.reshape(count, rows, width), grad_first, grad_second)


def solution(mesh):
    return jax.shard_map(
        shards,
        mesh=mesh,
        in_specs=(
            P("dp", "seq", None),
            P("dp", "seq", None),
            P("dp", "seq", None),
            P("seq", None, None),
            P("seq", None, None),
        ),
        out_specs=(P("dp", "seq", None), P("seq", None, None), P("seq", None, None)),
        check_vma=False,
    )
```

profile of v0, /device:TPU:96, one launch (start us, length us, event | category | flops | bytes accessed | tf_op | source)
XLA Modules:
  0.0 340.3 jit_solution(11930007781547913942)
XLA Ops:
  7.2 0.0 copy-start
  7.2 4.5 %multiply_convert_fusion = bf16[2,768,1024]{2,1,0:T(8,128)(2,1)S(1)} fusion(bf16[2,768,1024]{2,1,0:T(8,128)(2,1)} %param.6, bf16[2,768,1024]{2,1,0:T(8,128)(2,1)} %param.7), kind=kLoop, calls=%fused_computation | loop fusion | flops 6291456 | bytes 9437184 | tf_op jit(solution)/shard_map/convert_element_type | solution.py:14
  11.7 4.9 %copy.42 = bf16[2,3,256,1024]{3,0,1,2:T(2,128)(2,1)} copy(bf16[2,3,256,1024]{3,2,1,0:T(8,128)(2,1)S(1)} %bitcast.52) | data formatting | bytes 6291456 | tf_op jit(solution)/shard_map/reshape | solution.py:15
  16.6 0.0 copy-start.3
  16.6 11.0 %all-to-all-start = ((bf16[2,3,256,1024]{3,0,1,2:T(2,128)(2,1)}), bf16[2,3,256,1024]{3,0,1,2:T(2,128)(2,1)}, u32[]{:S(2)}, u32[]{:S(2)}) async-start(bf16[2,3,256,1024]{3,0,1,2:T(2,128)(2,1)} %copy.42), calls=%async_computation | async-start | bytes 6291456 | tf_op jit(solution)/shard_map/all_to_all | solution.py:17
  27.6 0.0 copy-done
  27.6 0.0 copy-done.3
  27.6 1.0 convert_bitcast_fusion
  28.6 5.0 %copy.53 = bf16[2,3,256,1024]{3,0,1,2:T(2,128)(2,1)} copy(bf16[2,3,256,1024]{3,2,0,1:T(8,128)(2,1)S(1)} %convert_bitcast_fusion) | data formatting | bytes 6291456 | tf_op jit(solution)/shard_map/convert_element_type | solution.py:13
  33.6 64.3 %all-to-all-done = bf16[2,3,256,1024]{3,0,1,2:T(2,128)(2,1)} async-done(((bf16[2,3,256,1024]{3,0,1,2:T(2,128)(2,1)}), bf16[2,3,256,1024]{3,0,1,2:T(2,128)(2,1)}, u32[]{:S(2)}, u32[]{:S(2)}) %all-to-all-start) | async-done | bytes 3145760 | tf_op jit(solution)/shard_map/all_to_all | solution.py:17
  97.9 9.4 %all-to-all-start.2 = ((bf16[2,3,256,1024]{3,0,1,2:T(2,128)(2,1)}), bf16[2,3,256,1024]{3,0,1,2:T(2,128)(2,1)}, u32[]{:S(2)}, u32[]{:S(2)}) async-start(bf16[2,3,256,1024]{3,0,1,2:T(2,128)(2,1)} %copy.53), calls=%async_computation.2 | async-start | bytes 6291456 | tf_op jit(solution)/shard_map/all_to_all | solution.py:16
  107.3 0.0 copy-start.4
  107.3 3.2 copy.44
  110.5 0.0 copy-start.1
  110.5 1.7 copy-done.1
  112.1 0.0 copy-done.4
  112.1 2.3 convert_bitcast_fusion.2
  114.5 5.0 %copy.46 = bf16[2,192,4,1024]{3,0,2,1:T(2,128)(2,1)} copy(bf16[2,192,4,1024]{3,1,0,2:T(8,128)(2,1)S(1)} %convert_bitcast_fusion.2) | data formatting | bytes 6291456 | tf_op jit(solution)/shard_map/convert_element_type | solution.py:21
  119.4 58.2 %all-to-all-done.2 = bf16[2,3,256,1024]{3,0,1,2:T(2,128)(2,1)} async-done(((bf16[2,3,256,1024]{3,0,1,2:T(2,128)(2,1)}), bf16[2,3,256,1024]{3,0,1,2:T(2,128)(2,1)}, u32[]{:S(2)}, u32[]{:S(2)}) %all-to-all-start.2) | async-done | bytes 3145760 | tf_op jit(solution)/shard_map/all_to_all | solution.py:16
  177.6 9.4 %all-to-all-start.1 = ((bf16[2,192,4,1024]{3,0,2,1:T(2,128)(2,1)}), bf16[2,192,4,1024]{3,0,2,1:T(2,128)(2,1)}, u32[]{:S(2)}, u32[]{:S(2)}) async-start(bf16[2,192,4,1024]{3,0,2,1:T(2,128)(2,1)} %copy.46), calls=%async_computation.1 | async-start | bytes 6291456 | tf_op jit(solution)/shard_map/all_to_all | solution.py:18
  187.0 0.3 all-reduce.3.cloned.1.call-start
  187.3 0.0 copy-start.2
  187.3 3.3 copy.54
  190.5 0.0 copy-done.2
  190.5 2.7 fusion.16
  193.2 64.1 %all-to-all-done.1 = bf16[2,192,4,1024]{3,0,2,1:T(2,128)(2,1)} async-done(((bf16[2,192,4,1024]{3,0,2,1:T(2,128)(2,1)}), bf16[2,192,4,1024]{3,0,2,1:T(2,128)(2,1)}, u32[]{:S(2)}, u32[]{:S(2)}) %all-to-all-start.1) | async-done | bytes 3145760 | tf_op jit(solution)/shard_map/all_to_all | solution.py:18
  257.3 3.1 copy.47
  260.4 2.9 copy.48
  263.4 5.5 %all_to_all.46 = bf16[2,3,256,1024]{3,2,0,1:T(8,128)(2,1)} reshape(bf16[2,3,64,4,1024]{4,3,2,0,1:T(4,128)(2,1)} %copy.48) | data formatting | bytes 6291456 | tf_op jit(solution)/shard_map/all_to_all | solution.py:18
  268.9 3.8 %fusion.13 = f32[3,256,256]{1,2,0:T(8,128)} fusion(bf16[2,3,256,1024]{3,2,0,1:T(8,128)(2,1)} %all_to_all.46, bf16[2,3,256,1024]{3,2,1,0:T(8,128)(2,1)S(1)} %bitcast.47), kind=kOutput, calls=%fused_computation.13 | convolution fusion | flops 805306368 | bytes 7077888 | tf_op jit(solution)/shard_map/nabd,nacd->abc/dot_general | solution.py:30
  272.7 0.0 all-reduce.3.cloned.1.call-update
  272.7 2.9 convert_bitcast_fusion.1
  275.6 2.2 copy.49
  277.8 51.2 %all-reduce.3.cloned.1.call-done = (f32[3,256,256]{1,2,0:T(8,128)}, f32[4,192,192]{2,1,0:T(8,128)}) async-done(((f32[3,256,256]{1,2,0:T(8,128)}, f32[4,192,192]{2,1,0:T(8,128)}), (f32[3,256,256]{1,2,0:T(8,128)}, f32[4,192,192]{2,1,0:T(8,128)})) %all-reduce.3.cloned.1.call-update) | async-done | bytes 1376272 | tf_op jit(solution)/shard_map/psum | solution.py:34
  329.1 2.3 copy.57
  331.3 2.1 copy.88
Async XLA Ops:
  7.2 20.4 %copy-start = (bf16[2,768,1024]{2,1,0:T(8,128)(2,1)S(1)}, bf16[2,768,1024]{2,1,0:T(8,128)(2,1)}, u32[]{:S(2)}) copy-start(bf16[2,768,1024]{2,1,0:T(8,128)(2,1)} %param.5) | copy-start | bytes 9437188
  16.6 11.0 %copy-start.3 = (bf16[3,256,256]{2,1,0:T(8,128)(2,1)S(1)}, bf16[3,256,256]{2,1,0:T(8,128)(2,1)}, u32[]{:S(2)}) copy-start(bf16[3,256,256]{2,1,0:T(8,128)(2,1)} %param.8) | copy-start | bytes 1179652
  16.6 81.3 %all-to-all-start = ((bf16[2,3,256,1024]{3,0,1,2:T(2,128)(2,1)}), bf16[2,3,256,1024]{3,0,1,2:T(2,128)(2,1)}, u32[]{:S(2)}, u32[]{:S(2)}) async-start(bf16[2,3,256,1024]{3,0,1,2:T(2,128)(2,1)} %copy.42), calls=%async_computation | async-start | bytes 6291456 | tf_op jit(solution)/shard_map/all_to_all | solution.py:17
  97.9 79.7 %all-to-all-start.2 = ((bf16[2,3,256,1024]{3,0,1,2:T(2,128)(2,1)}), bf16[2,3,256,1024]{3,0,1,2:T(2,128)(2,1)}, u32[]{:S(2)}, u32[]{:S(2)}) async-start(bf16[2,3,256,1024]{3,0,1,2:T(2,128)(2,1)} %copy.53), calls=%async_computation.2 | async-start | bytes 6291456 | tf_op jit(solution)/shard_map/all_to_all | solution.py:16
  107.3 4.8 %copy-start.4 = (bf16[4,192,192]{2,1,0:T(8,128)(2,1)S(1)}, bf16[4,192,192]{2,1,0:T(8,128)(2,1)}, u32[]{:S(2)}) copy-start(bf16[4,192,192]{2,1,0:T(8,128)(2,1)} %param.9) | copy-start | bytes 884740
  110.5 1.7 copy-start.1
  177.6 79.7 %all-to-all-start.1 = ((bf16[2,192,4,1024]{3,0,2,1:T(2,128)(2,1)}), bf16[2,192,4,1024]{3,0,2,1:T(2,128)(2,1)}, u32[]{:S(2)}, u32[]{:S(2)}) async-start(bf16[2,192,4,1024]{3,0,2,1:T(2,128)(2,1)} %copy.46), calls=%async_computation.1 | async-start | bytes 6291456 | tf_op jit(solution)/shard_map/all_to_all | solution.py:18
  187.0 142.1 %all-reduce.3.cloned.1.call-start = ((), (), s32[]{:S(2)}) async-start(), calls=%async_computation.3 | async-start | bytes 3145728 | tf_op jit(solution)/shard_map/psum | solution.py:34
  187.3 3.3 copy-start.2
Sparse Core Ops, SparseCore 0:
  272.8 56.1 all-reduce.2
where the time goes:
time: 343 us; the launch traced here: 340 us
  waiting for transfers between devices  238 us (69%)
  local copies, waits for them, and re-layouts  41.1 us (12%)
  starting transfers between devices  30 us (9%)
  between operations  14.2 us (4%)
  matrix products  12.7 us (4%)
  other arithmetic  4.52 us (1%)
    all_to_all x1, waiting for transfers between devices, shards(): lax.all_to_all(scaled, 'seq', split_axis=2, concat_axis=1, tiled=True)  64.3 us
    all_to_all x1, waiting for transfers between devices, shards(): lax.all_to_all(jnp.einsum('cae,necd->nacd', second_blocks, scaled_cols, p...  64.1 us
    all_to_all x1, waiting for transfers between devices, shards(): lax.all_to_all(mixed, 'seq', split_axis=2, concat_axis=1, tiled=True)  58.2 us
    psum x1, waiting for transfers between devices, shards(): grad_first, grad_second = lax.psum((grad_first, grad_second), 'dp')  51.2 us
    all_to_all x3, local copies, waits for them, and re-layouts, shards(): lax.all_to_all(jnp.einsum('cae,necd->nacd', second_blocks, scaled_cols, p...  11.6 us
    all_to_all x1, starting transfers between devices, shards(): lax.all_to_all(scaled, 'seq', split_axis=2, concat_axis=1, tiled=True)  11 us
    all_to_all x1, starting transfers between devices, shards(): lax.all_to_all(mixed, 'seq', split_axis=2, concat_axis=1, tiled=True)  9.36 us
    all_to_all x1, starting transfers between devices, shards(): lax.all_to_all(jnp.einsum('cae,necd->nacd', second_blocks, scaled_cols, p...  9.35 us
  transfers between devices with their start and end apart: 4, of which 4 were waited for; matrix products, arithmetic and copies ran while one was open for 8% of the time, Pallas kernels for 0%

commit v1 on v0

v1 whole, which is shorter than its diff:
```python
import jax
import jax.numpy as jnp
from jax import lax
from jax.sharding import PartitionSpec as P

X, Z, C = 4, 8, 2
F32, BF16 = jnp.float32, jnp.bfloat16


def spot(x, z, c):
    return ((x % X) * Z + z % Z) * C + c % C


def moved(dx, dz, dc):
    return [
        (spot(x, z, c), spot(x + dx, z + dz, c + dc))
        for x in range(X)
        for z in range(Z)
        for c in range(C)
    ]


ROWS = [[spot(x, z, c) for x in range(X)] for z in range(Z) for c in range(C)]
STEPS = (4, 1, 7, 2, 6, 3, 5)


def hop(array, dz):
    return lax.ppermute(array, "seq", moved(0, dz, 0))


def swap(array):
    return lax.ppermute(array, "seq", moved(0, 0, 1))


def across(array):
    return lax.all_to_all(array, "seq", 0, 0, axis_index_groups=ROWS, tiled=True)


def after(array, earlier):
    return lax.optimization_barrier((array, earlier))[0]


def along(pieces, earlier):
    got = [pieces[0]] + [None] * (Z - 1)
    for k in STEPS:
        piece = pieces[k] if earlier is None else after(pieces[k], earlier[k])
        got[k] = hop(piece, k)
    return got


def dp_sum(array):
    n = 4
    me = lax.axis_index("dp")
    parts = array.reshape((n, -1) + array.shape[1:])
    total = lax.dynamic_index_in_dim(parts, me, 0, keepdims=False)
    for k in range(1, n):
        part = lax.dynamic_index_in_dim(parts, (me + k) % n, 0, keepdims=False).astype(BF16)
        total += lax.ppermute(part, "dp", [(i, (i + k) % n) for i in range(n)]).astype(F32)
    out = jnp.zeros_like(parts)
    out = lax.dynamic_update_index_in_dim(out, total, me, 0)
    sent = total.astype(BF16)
    for k in range(1, n):
        part = lax.ppermute(sent, "dp", [(i, (i + k) % n) for i in range(n)]).astype(F32)
        out = lax.dynamic_update_index_in_dim(out, part, (me - k) % n, 0)
    return out.reshape(array.shape)


def shards(values, gates, grad_out, first_blocks, second_blocks):
    count, rows, width = values.shape
    A3, B = first_blocks.shape[:2]
    C8 = B // (X * Z)
    C4, A = second_blocks.shape[:2]
    here = lax.axis_index("seq")
    core, z = here % C, (here // C) % Z
    up = (z + jnp.arange(Z)) % Z
    down = (z - jnp.arange(Z)) % Z

    view = (A3, X, Z, C8, width)
    moved_g, earlier = [], None
    for n in range(count):
        a, b = gates[n].reshape(view), grad_out[n].reshape(view)
        pieces = []
        for k in range(Z):
            at = (z + k) % Z
            p = lax.dynamic_index_in_dim(a, at, 2, keepdims=False).astype(F32)
            q = lax.dynamic_index_in_dim(b, at, 2, keepdims=False).astype(F32)
            pieces.append((p * q).astype(BF16))
        earlier = along(pieces, earlier)
        moved_g.append(earlier)

    first = first_blocks.reshape(A3, B, X, Z, C8)
    first_up = jnp.take(first, up, axis=3).reshape(A3, B, B)
    inputs = values.reshape(count, A3, B, width)
    across_u = []
    for n in range(count):
        mixed = jnp.einsum("abd,abc->acd", inputs[n], first_up, preferred_element_type=F32)
        mixed = mixed.astype(BF16).reshape(A3, X, Z, C8, width)
        across_u.append(across(mixed.transpose(1, 0, 2, 3, 4)))

    second = second_blocks.reshape(C4, A // (C * A3), C, A3, A)
    mine = lax.dynamic_index_in_dim(second, core, 2, keepdims=False)
    other = swap(lax.dynamic_index_in_dim(second, 1 - core, 2, keepdims=False))
    pair = jnp.where(core == 0, jnp.stack([mine, other]), jnp.stack([other, mine]))
    pair = pair.reshape(C8, X, Z, A3, X, Z, C, A3)
    pair = jnp.take(jnp.take(pair, up, axis=2), down, axis=5)
    pair = jnp.where(core == 0, pair, pair[:, :, :, :, :, :, ::-1])
    pair = pair.transpose(0, 1, 2, 3, 6, 4, 5, 7).reshape(C8, A // C, C, A // C)

    cols_g = []
    for n in range(count):
        own = across(jnp.stack(moved_g[n]).transpose(2, 0, 1, 3, 4))
        own = own.reshape(A // C, C8, width)
        cols_g.append(jnp.stack([own, swap(own)]))

    moved_u = []
    for n in range(count):
        part = across_u[n].reshape(X, A3, Z, C8, width)
        earlier = along([part[:, :, k] for k in range(Z)], earlier)
        moved_u.append(earlier)

    across_v = []
    for n in range(count):
        inner = jnp.einsum("came,mecd->acd", pair, cols_g[n], preferred_element_type=F32)
        across_v.append(across(inner.astype(BF16).reshape(X, Z, A3, C8, width)))

    moved_v = []
    for n in range(count):
        earlier = along([across_v[n][:, k] for k in range(Z)], earlier)
        moved_v.append(earlier)

    grad_second = 0
    for n in range(count):
        cols_u = jnp.stack(moved_u[n]).reshape(A // C, C8, width)
        grad_second += jnp.einsum("acd,mecd->came", cols_u, cols_g[n], preferred_element_type=F32)
    grad_second = grad_second.reshape(C, C4, A // C, C, A // C)
    mine = lax.dynamic_index_in_dim(grad_second, core, 0, keepdims=False)
    other = swap(lax.dynamic_index_in_dim(grad_second, 1 - core, 0, keepdims=False))
    other = other[:, :, ::-1]
    pair = jnp.where(core == 0, jnp.stack([mine, other]), jnp.stack([other, mine]))
    pair = jnp.where(core == 0, pair, pair[:, :, :, ::-1])
    pair = pair.reshape(C, C4, Z, X, A3, C, X, Z, A3)
    pair = jnp.take(jnp.take(pair, down, axis=2), down, axis=7)
    pair = pair.transpose(1, 3, 2, 0, 4, 6, 7, 5, 8).reshape(C4, A, A)
    grad_second = lax.psum(pair, "dp")

    grad_first = 0
    results = []
    for n in range(count):
        inner = jnp.zeros((A3, X, Z, C8, width), BF16)
        for k in range(Z):
            piece = moved_v[n][k].transpose(1, 0, 2, 3)
            inner = lax.dynamic_update_index_in_dim(inner, piece, (z - k) % Z, 2)
        inner = inner.reshape(A3, B, width)
        grad_first += jnp.einsum("abd,acd->abc", inputs[n], inner, preferred_element_type=F32)
        results.append(
            jnp.einsum("abc,acd->abd", first_blocks, inner, preferred_element_type=F32).astype(BF16)
        )
    grad_values = jnp.stack(results).reshape(count, rows, width)
    grad_first = dp_sum(grad_first.reshape(A3 * B, B)).reshape(A3, B, B)
    return grad_values, grad_first, grad_second


def solution(mesh):
    return jax.shard_map(
        shards,
        mesh=mesh,
        in_specs=(
            P("dp", "seq", None),
            P("dp", "seq", None),
            P("dp", "seq", None),
            P("seq", None, None),
            P("seq", None, None),
        ),
        out_specs=(P("dp", "seq", None), P("seq", None, None), P("seq", None, None)),
        check_vma=False,
    )
```

time: 343 us -> 650 us (1.90); the launches traced: 340 us -> 638 us
  local copies, waits for them, and re-layouts: 41.1 us -> 330 us
  waiting for transfers between devices: 238 us -> 90 us
  starting transfers between devices: 30 us -> 143 us
  other arithmetic: 4.52 us -> 48.5 us
    all_to_all x3 -> x6, waiting for transfers between devices: 187 us -> 2.72 us  [across(): lax.all_to_all(array, 'seq', 0, 0, axis_index_groups=ROWS, tiled=True)]
    ppermute x0 -> x52, starting transfers between devices: none -> 117 us  [the longest x42 107 us: hop(): return lax.ppermute(array, 'seq', moved(0, dz, 0))]
    reshape x1 -> x8, local copies, waits for them, and re-layouts: 4.9 us -> 116 us  [the longest x2 67.2 us: shards(): pair = pair.reshape(C, C4, Z, X, A3, C, X, Z, A3)]
    select_n x0 -> x6, local copies, waits for them, and re-layouts: none -> 88.2 us  [the longest x2 63 us: shards(): pair = jnp.take(jnp.take(pair, down, axis=2), down, axis=7)]
    ppermute x0 -> x52, waiting for transfers between devices: none -> 87.2 us  [the longest x42 79.7 us: hop(): return lax.ppermute(array, 'seq', moved(0, dz, 0))]
    psum x1, waiting for transfers between devices: 51.2 us -> 0.02 us  [shards(): grad_second = lax.psum(pair, 'dp')]
    gather x0 -> x6, local copies, waits for them, and re-layouts: none -> 35.4 us  [the longest x2 23.3 us: shards(): pair = jnp.take(jnp.take(pair, down, axis=2), down, axis=7)]
    select_n x0 -> x9, other arithmetic: none -> 31.2 us  [the longest x2 21.2 us: shards(): pair = jnp.take(jnp.take(pair, down, axis=2), down, axis=7)]
  transfers between devices with their start and end apart: 4 -> 59, of which waited for: 4 -> 21; matrix products, arithmetic and copies ran while one was open for 8% -> 59% of each run, Pallas kernels for 0% -> 0%
where the time goes in v1:
time: 650 us; the launch traced here: 638 us
  local copies, waits for them, and re-layouts  330 us (51%)
  starting transfers between devices  143 us (22%)
  waiting for transfers between devices  90 us (14%)
  other arithmetic  48.5 us (7%)
  between operations  15.2 us (2%)
  matrix products  10.6 us (2%)
    ppermute x42, starting transfers between devices, hop(): return lax.ppermute(array, 'seq', moved(0, dz, 0))  107 us
    ppermute x42, waiting for transfers between devices, hop(): return lax.ppermute(array, 'seq', moved(0, dz, 0))  79.7 us
    reshape x2, local copies, waits for them, and re-layouts, shards(): pair = pair.reshape(C, C4, Z, X, A3, C, X, Z, A3)  67.2 us
    select_n x2, local copies, waits for them, and re-layouts, shards(): pair = jnp.take(jnp.take(pair, down, axis=2), down, axis=7)  63 us
    unnamed x83, local copies, waits for them, and re-layouts  36 us
    reshape x1, local copies, waits for them, and re-layouts, shards(): pair = pair.transpose(1, 3, 2, 0, 4, 6, 7, 5, 8).reshape(C4, A, A)  33.7 us
    all_to_all x6, starting transfers between devices, across(): lax.all_to_all(array, 'seq', 0, 0, axis_index_groups=ROWS, tiled=True)  26 us
    gather x2, local copies, waits for them, and re-layouts, shards(): pair = jnp.take(jnp.take(pair, down, axis=2), down, axis=7)  23.3 us
  transfers between devices with their start and end apart: 59, of which 21 were waited for; matrix products, arithmetic and copies ran while one was open for 59% of the time, Pallas kernels for 0%

profile of v1, /device:TPU:96, one launch (start us, length us, event | category | flops | bytes accessed | tf_op | source)
XLA Modules:
  0.0 637.7 jit_solution(10872751307863949325)
XLA Ops:
  16.4 4.3 all-to-all-start.2
  20.7 4.0 fusion.51
  28.6 3.0 fusion.19
  32.3 5.7 collective-permute-start.4
  46.0 2.8 fusion.27
  48.8 3.0 collective-permute-start
  53.5 3.6 select_n.401
  57.1 11.6 %copy.186 = bf16[8,4,8,3,4,8,2,3]{5,0,6,7,3,1,4,2:T(8,128)(2,1)} copy(bf16[8,4,8,3,4,8,2,3]{2,1,7,6,5,4,3,0:T(4,128)(2,1)} %select_n.401) | data formatting | bytes 589824 | tf_op jit(solution)/shard_map/jit(_where)/select_n | solution.py:103
  68.7 5.7 gather_fusion
  74.4 5.1 select_bitcast_fusion.3
  79.5 9.6 %copy.187 = bf16[8,4,8,3,4,8,2,3]{2,0,7,6,5,4,3,1:T(8,128)(2,1)} copy(bf16[8,4,8,3,4,8,2,3]{5,0,6,7,3,1,4,2:T(8,128)(2,1)} %select_bitcast_fusion.3) | data formatting | bytes 589824 | tf_op jit(solution)/shard_map/jit(_take)/select_n | solution.py:105
  89.1 5.7 gather_fusion.1
  94.8 2.9 select_bitcast_fusion.2
  97.6 3.6 fusion
  101.3 12.1 %copy.188 = bf16[8,4,8,3,2,4,8,3]{0,4,7,6,5,3,2,1:T(2,128)(2,1)} copy(bf16[8,4,8,3,2,4,8,3]{2,0,7,4,5,3,1,6:T(8,128)(2,1)} %fusion) | data formatting | bytes 589824 | tf_op jit(solution)/shard_map/transpose | solution.py:107
  113.4 9.2 %copy.189 = bf16[8,96,2,96]{3,1,2,0:T(8,128)(2,1)} copy(bf16[8,96,2,96]{0,2,3,1:T(2,128)(2,1)} %bitcast.456) | data formatting | bytes 589824 | tf_op jit(solution)/shard_map/reshape | solution.py:107
  122.6 2.8 collective-permute-start.1
  126.4 7.3 %collective-permute-done.1 = bf16[3,4,8,1024]{3,2,1,0:T(8,128)(2,1)S(1)} collective-permute-done((bf16[3,4,8,1024]{3,2,1,0:T(8,128)(2,1)S(1)}, bf16[3,4,8,1024]{3,2,1,0:T(8,128)(2,1)S(1)}, u32[]{:S(2)}, u32[]{:S(2)}) %collective-permute-start.1) | collective-permute-done | bytes 196640 | tf_op jit(solution)/shard_map/ppermute | solution.py:28
  136.0 12.4 %collective-permute-done.2 = bf16[3,4,8,1024]{3,2,1,0:T(8,128)(2,1)S(1)} collective-permute-done((bf16[3,4,8,1024]{3,2,1,0:T(8,128)(2,1)S(1)}, bf16[3,4,8,1024]{3,2,1,0:T(8,128)(2,1)S(1)}, u32[]{:S(2)}, u32[]{:S(2)}) %collective-permute-start.2) | collective-permute-done | bytes 196640 | tf_op jit(solution)/shard_map/ppermute | solution.py:28
  148.4 2.7 collective-permute-start.9
  157.9 4.9 collective-permute-start.17
  166.3 2.6 collective-permute-start.29
  169.6 4.5 all-to-all-start.3
  176.7 4.3 collective-permute-done.17
  184.2 3.5 collective-permute-done.25
  189.4 5.8 collective-permute-done.29
  197.8 2.7 copy.225
  201.6 4.5 all-to-all-start
  209.2 3.1 collective-permute-start.14
  213.0 5.3 collective-permute-start.22
  224.4 2.7 all-to-all-done
  227.1 3.6 all-to-all-start.4
  233.1 3.5 collective-permute-done.18
  236.7 5.7 collective-permute-start.11
  242.4 2.7 collective-permute-start.15
  245.1 7.2 %collective-permute-start.19 = (bf16[4,3,8,1024]{3,2,1,0:T(8,128)(2,1)}, bf16[4,3,8,1024]{3,2,1,0:T(8,128)(2,1)}, u32[]{:S(2)}, u32[]{:S(2)}) collective-permute-start(bf16[4,3,8,1024]{3,2,1,0:T(8,128)(2,1)} %get-tuple-element.48), channel_id=1, source_target_pairs={{0,6},{1,7},{2,8},{3,9},{4,10},{5,11},{6,12},{7,13},{8,14},{9,15},... | collective-permute-start | bytes 589832 | tf_op jit(solution)/shard_map/ppermute | solution.py:28
  253.2 3.2 collective-permute-start.27
  271.4 7.6 %collective-permute-start.31 = (bf16[4,3,8,1024]{3,2,1,0:T(8,128)(2,1)S(1)}, bf16[4,3,8,1024]{3,2,1,0:T(8,128)(2,1)S(1)}, u32[]{:S(2)}, u32[]{:S(2)}) collective-permute-start(bf16[4,3,8,1024]{3,2,1,0:T(8,128)(2,1)S(1)} %copy-done.22), channel_id=1, source_target_pairs={{0,12},{1,13},{2,14},{3,15},{4,0},{5,1},{6,2},{7,3},{8,4},{9,5},{1... | collective-permute-start | bytes 589832 | tf_op jit(solution)/shard_map/ppermute | solution.py:28
  283.1 4.0 collective-permute-done.31
  291.1 2.8 fusion.9
  297.7 4.3 all-to-all-start.1
  307.4 27.4 %reshape.314 = f32[2,4,8,4,3,2,4,8,3]{8,7,6,4,3,2,5,1,0:T(8,128)} reshape(f32[2,4,96,2,96]{4,2,3,1,0:T(8,128)S(1)} %reverse_select_fusion.1) | data formatting | bytes 1179648 | tf_op jit(solution)/shard_map/reshape | solution.py:141
  334.8 39.9 %copy.235 = f32[2,4,8,4,3,2,4,8,3]{7,6,8,5,4,3,2,1,0:T(4,128)} copy(f32[2,4,8,4,3,2,4,8,3]{8,7,6,4,3,2,5,1,0:T(8,128)} %reshape.314) | data formatting | bytes 1179648 | tf_op jit(solution)/shard_map/reshape | solution.py:141
  374.6 11.5 %gather_fusion.3 = f32[8,2,4,4,3,2,4,8,3]{7,6,8,5,4,3,2,1,0:T(4,128)} fusion(f32[2,4,8,4,3,2,4,8,3]{7,6,8,5,4,3,2,1,0:T(4,128)} %copy.235, s32[1024]{0:T(1024)S(1)} %pad_clamp_fusion), kind=kCustom, calls=%fused_computation.3 | custom fusion | bytes 1179680 | tf_op jit(solution)/shard_map/jit(_take)/gather | solution.py:142
  386.2 10.6 %select_bitcast_fusion.1 = f32[2,4,8,4,3,2,4,8,3]{7,6,8,5,4,3,1,0,2:T(4,128)} fusion(f32[8,2,4,4,3,2,4,8,3]{7,6,8,5,4,3,2,1,0:T(4,128)} %gather_fusion.3, pred[8]{0:T(512)(128)(4,1)S(1)} %get-tuple-element.128), kind=kLoop, calls=%fused_computation.6 | loop fusion | flops 147456 | bytes 1179656 | tf_op jit(solution)/shard_map/jit(_take)/select_n | solution.py:142
  396.8 14.3 %copy.236 = f32[2,4,8,4,3,2,4,8,3]{2,3,5,4,8,6,1,0,7:T(4,128)} copy(f32[2,4,8,4,3,2,4,8,3]{7,6,8,5,4,3,1,0,2:T(4,128)} %select_bitcast_fusion.1) | data formatting | bytes 1179648 | tf_op jit(solution)/shard_map/jit(_take)/select_n | solution.py:142
  411.0 11.8 %gather_fusion.4 = f32[8,2,4,8,4,3,2,4,3]{3,4,6,5,8,7,2,1,0:T(4,128)} fusion(f32[2,4,8,4,3,2,4,8,3]{2,3,5,4,8,6,1,0,7:T(4,128)} %copy.236, s32[1024]{0:T(1024)S(1)} %pad_clamp_fusion), kind=kCustom, calls=%fused_computation.4 | custom fusion | bytes 1179680 | tf_op jit(solution)/shard_map/jit(_take)/gather | solution.py:142
  422.8 4.8 all-to-all-start.5
  427.6 10.6 %select_bitcast_fusion = f32[4,4,8,2,3,4,8,2,3]{2,1,7,4,8,5,0,3,6:T(4,128)} fusion(f32[8,2,4,8,4,3,2,4,3]{3,4,6,5,8,7,2,1,0:T(4,128)} %gather_fusion.4, pred[8]{0:T(512)(128)(4,1)S(1)} %get-tuple-element.128), kind=kLoop, calls=%fused_computation.5 | loop fusion | flops 147456 | bytes 1179656 | tf_op jit(solution)/shard_map/jit(_take)/select_n | solution.py:142
  438.3 48.7 %copy.237 = f32[4,4,8,2,3,4,8,2,3]{8,7,6,5,4,3,2,1,0:T(2,128)} copy(f32[4,4,8,2,3,4,8,2,3]{2,1,7,4,8,5,0,3,6:T(4,128)} %select_bitcast_fusion) | data formatting | bytes 1179648 | tf_op jit(solution)/shard_map/jit(_take)/select_n | solution.py:142
  486.9 33.7 %reshape.315 = f32[4,192,192]{2,1,0:T(8,128)} reshape(f32[4,4,8,2,3,4,8,2,3]{8,7,6,5,4,3,2,1,0:T(2,128)} %copy.237) | data formatting | bytes 1179648 | tf_op jit(solution)/shard_map/reshape | solution.py:143
  522.7 2.5 collective-permute-start.16
  529.3 2.5 collective-permute-start.28
  537.0 5.1 collective-permute-done.16
  542.1 10.9 %collective-permute-done.20 = bf16[4,3,8,1024]{3,2,1,0:T(8,128)(2,1)} collective-permute-done((bf16[4,3,8,1024]{3,2,1,0:T(8,128)(2,1)}, bf16[4,3,8,1024]{3,2,1,0:T(8,128)(2,1)}, u32[]{:S(2)}, u32[]{:S(2)}) %collective-permute-start.20) | collective-permute-done | bytes 196640 | tf_op jit(solution)/shard_map/ppermute | solution.py:28
  552.9 8.1 %collective-permute-start.38 = (bf16[4,3,8,1024]{3,2,1,0:T(8,128)(2,1)S(1)}, bf16[4,3,8,1024]{3,2,1,0:T(8,128)(2,1)S(1)}, u32[]{:S(2)}, u32[]{:S(2)}) collective-permute-start(bf16[4,3,8,1024]{3,2,1,0:T(8,128)(2,1)S(1)} %get-tuple-element.66), channel_id=1, source_target_pairs={{0,2},{1,3},{2,4},{3,5},{4,6},{5,7},{6,8},{7,9},{8,10},{9,11},{10,... | collective-permute-start | bytes 589832 | tf_op jit(solution)/shard_map/ppermute | solution.py:28
  562.1 5.8 collective-permute-start.40
  577.1 3.3 collective-permute-start.42
  581.0 4.1 collective-permute-start.43
  585.5 3.9 collective-permute-done.41
  589.5 7.6 %collective-permute-done.42 = bf16[4,3,8,1024]{3,2,1,0:T(8,128)(2,1)S(1)} collective-permute-done((bf16[4,3,8,1024]{3,2,1,0:T(8,128)(2,1)S(1)}, bf16[4,3,8,1024]{3,2,1,0:T(8,128)(2,1)S(1)}, u32[]{:S(2)}, u32[]{:S(2)}) %collective-permute-start.42) | collective-permute-done | bytes 196640 | tf_op jit(solution)/shard_map/ppermute | solution.py:28
  597.1 4.8 collective-permute-done.43
  610.1 2.5 collective-permute-start.47
  622.5 5.4 collective-permute-done.48
  (239 shorter events, 136.7 us)
Async XLA Ops:
  10.1 38.7 %collective-permute-start.8 = (bf16[4,32,3,192]{3,1,2,0:T(8,128)(2,1)}, bf16[4,32,3,192]{3,1,2,0:T(8,128)(2,1)}, u32[]{:S(2)}, u32[]{:S(2)}) collective-permute-start(bf16[4,32,3,192]{3,1,2,0:T(8,128)(2,1)} %bitcast.452), channel_id=1, source_target_pairs={{0,1},{1,0},{2,3},{3,2},{4,5},{5,4},{6,7},{7,6},{8,9},{9,8},{10,11... | collective-permute-start | bytes 442376 | tf_op jit(solution)/shard_map/ppermute | solution.py:32
  13.9 26.8 %copy-start = (bf16[1,768,1024]{2,1,0:T(8,128)(2,1)}, bf16[1,768,1024]{2,1,0:T(8,128)(2,1)S(1)}, u32[]{:S(2)}) copy-start(bf16[1,768,1024]{2,1,0:T(8,128)(2,1)S(1)} %get-tuple-element.73) | copy-start | bytes 4718596
  16.4 153.2 %all-to-all-start.2 = ((bf16[4,3,8,8,1024]{4,3,1,2,0:T(8,128)(2,1)}), bf16[4,3,8,8,1024]{4,3,1,2,0:T(8,128)(2,1)S(1)}, u32[]{:S(2)}, u32[]{:S(2)}) async-start(bf16[4,3,8,8,1024]{4,3,1,2,0:T(8,128)(2,1)} %bitcast.469), calls=%async_computation.2 | async-start | bytes 3145728 | tf_op jit(solution)/shard_map/all_to_all | solution.py:36
  28.5 125.6 %collective-permute-start.6 = (bf16[3,4,8,1024]{3,2,1,0:T(8,128)(2,1)}, bf16[3,4,8,1024]{3,2,1,0:T(8,128)(2,1)}, u32[]{:S(2)}, u32[]{:S(2)}) collective-permute-start(bf16[3,4,8,1024]{3,2,1,0:T(8,128)(2,1)} %fusion.20), channel_id=1, source_target_pairs={{0,14},{1,15},{2,0},{3,1},{4,2},{5,3},{6,4},{7,5},{8,6},{9,7},{10,... | collective-permute-start | bytes 589832 | tf_op jit(solution)/shard_map/ppermute | solution.py:28
  31.6 121.5 %collective-permute-start.5 = (bf16[3,4,8,1024]{3,2,1,0:T(8,128)(2,1)}, bf16[3,4,8,1024]{3,2,1,0:T(8,128)(2,1)}, u32[]{:S(2)}, u32[]{:S(2)}) collective-permute-start(bf16[3,4,8,1024]{3,2,1,0:T(8,128)(2,1)} %get-tuple-element.82), channel_id=1, source_target_pairs={{0,12},{1,13},{2,14},{3,15},{4,0},{5,1},{6,2},{7,3},{8,4},{9,5},{1... | collective-permute-start | bytes 589832 | tf_op jit(solution)/shard_map/ppermute | solution.py:28
  32.3 119.8 %collective-permute-start.4 = (bf16[3,4,8,1024]{3,2,1,0:T(8,128)(2,1)}, bf16[3,4,8,1024]{3,2,1,0:T(8,128)(2,1)}, u32[]{:S(2)}, u32[]{:S(2)}) collective-permute-start(bf16[3,4,8,1024]{3,2,1,0:T(8,128)(2,1)} %get-tuple-element.83), channel_id=1, source_target_pairs={{0,10},{1,11},{2,12},{3,13},{4,14},{5,15},{6,0},{7,1},{8,2},{9,3},... | collective-permute-start | bytes 589832 | tf_op jit(solution)/shard_map/ppermute | solution.py:28
  38.0 113.2 %collective-permute-start.3 = (bf16[3,4,8,1024]{3,2,1,0:T(8,128)(2,1)}, bf16[3,4,8,1024]{3,2,1,0:T(8,128)(2,1)}, u32[]{:S(2)}, u32[]{:S(2)}) collective-permute-start(bf16[3,4,8,1024]{3,2,1,0:T(8,128)(2,1)} %get-tuple-element.84), channel_id=1, source_target_pairs={{0,8},{1,9},{2,10},{3,11},{4,12},{5,13},{6,14},{7,15},{8,0},{9,1},... | collective-permute-start | bytes 589832 | tf_op jit(solution)/shard_map/ppermute | solution.py:28
  48.8 73.8 %collective-permute-start = (bf16[3,4,8,1024]{3,2,1,0:T(8,128)(2,1)}, bf16[3,4,8,1024]{3,2,1,0:T(8,128)(2,1)}, u32[]{:S(2)}, u32[]{:S(2)}) collective-permute-start(bf16[3,4,8,1024]{3,2,1,0:T(8,128)(2,1)} %get-tuple-element.87), channel_id=1, source_target_pairs={{0,2},{1,3},{2,4},{3,5},{4,6},{5,7},{6,8},{7,9},{8,10},{9,11},{10,... | collective-permute-start | bytes 589832 | tf_op jit(solution)/shard_map/ppermute | solution.py:28
  113.4 12.0 %copy-start.9 = (bf16[8,3,4,8,1024]{4,3,2,1,0:T(8,128)(2,1)S(1)}, bf16[8,3,4,8,1024]{4,3,2,1,0:T(8,128)(2,1)}, u32[]{:S(2)}) copy-start(bf16[8,3,4,8,1024]{4,3,2,1,0:T(8,128)(2,1)} %fusion.13) | copy-start | bytes 4718596
  113.4 20.3 %copy-start.17 = (bf16[3,4,8,1024]{3,2,1,0:T(8,128)(2,1)S(1)}, bf16[3,4,8,1024]{3,2,1,0:T(8,128)(2,1)}, u32[]{:S(2)}) copy-start(bf16[3,4,8,1024]{3,2,1,0:T(8,128)(2,1)} %get-tuple-element.85) | copy-start | bytes 589828
  122.6 11.1 %collective-permute-start.1 = (bf16[3,4,8,1024]{3,2,1,0:T(8,128)(2,1)S(1)}, bf16[3,4,8,1024]{3,2,1,0:T(8,128)(2,1)S(1)}, u32[]{:S(2)}, u32[]{:S(2)}) collective-permute-start(bf16[3,4,8,1024]{3,2,1,0:T(8,128)(2,1)S(1)} %copy-done.18), channel_id=1, source_target_pairs={{0,4},{1,5},{2,6},{3,7},{4,8},{5,9},{6,10},{7,11},{8,12},{9,13},{1... | collective-permute-start | bytes 589832 | tf_op jit(solution)/shard_map/ppermute | solution.py:28
  133.7 14.7 %collective-permute-start.2 = (bf16[3,4,8,1024]{3,2,1,0:T(8,128)(2,1)S(1)}, bf16[3,4,8,1024]{3,2,1,0:T(8,128)(2,1)S(1)}, u32[]{:S(2)}, u32[]{:S(2)}) collective-permute-start(bf16[3,4,8,1024]{3,2,1,0:T(8,128)(2,1)S(1)} %copy-done.17), channel_id=1, source_target_pairs={{0,6},{1,7},{2,8},{3,9},{4,10},{5,11},{6,12},{7,13},{8,14},{9,15},... | collective-permute-start | bytes 589832 | tf_op jit(solution)/shard_map/ppermute | solution.py:28
  148.4 17.9 %collective-permute-start.9 = (bf16[3,4,8,1024]{3,2,1,0:T(8,128)(2,1)}, bf16[3,4,8,1024]{3,2,1,0:T(8,128)(2,1)S(1)}, u32[]{:S(2)}, u32[]{:S(2)}) collective-permute-start(bf16[3,4,8,1024]{3,2,1,0:T(8,128)(2,1)} %get-tuple-element.38), channel_id=1, source_target_pairs={{0,2},{1,3},{2,4},{3,5},{4,6},{5,7},{6,8},{7,9},{8,10},{9,11},{10,... | collective-permute-start | bytes 589832 | tf_op jit(solution)/shard_map/ppermute | solution.py:28
  155.0 11.3 %copy-start.20 = (bf16[3,4,8,1024]{3,2,1,0:T(8,128)(2,1)S(1)}, bf16[3,4,8,1024]{3,2,1,0:T(8,128)(2,1)}, u32[]{:S(2)}) copy-start(bf16[3,4,8,1024]{3,2,1,0:T(8,128)(2,1)} %get-tuple-element.58) | copy-start | bytes 589828
  156.3 18.2 %collective-permute-start.13 = (bf16[3,4,8,1024]{3,2,1,0:T(8,128)(2,1)}, bf16[3,4,8,1024]{3,2,1,0:T(8,128)(2,1)}, u32[]{:S(2)}, u32[]{:S(2)}) collective-permute-start(bf16[3,4,8,1024]{3,2,1,0:T(8,128)(2,1)} %get-tuple-element.42), channel_id=1, source_target_pairs={{0,4},{1,5},{2,6},{3,7},{4,8},{5,9},{6,10},{7,11},{8,12},{9,13},{1... | collective-permute-start | bytes 589832 | tf_op jit(solution)/shard_map/ppermute | solution.py:28
  157.9 23.1 %collective-permute-start.17 = (bf16[3,4,8,1024]{3,2,1,0:T(8,128)(2,1)}, bf16[3,4,8,1024]{3,2,1,0:T(8,128)(2,1)}, u32[]{:S(2)}, u32[]{:S(2)}) collective-permute-start(bf16[3,4,8,1024]{3,2,1,0:T(8,128)(2,1)} %get-tuple-element.46), channel_id=1, source_target_pairs={{0,6},{1,7},{2,8},{3,9},{4,10},{5,11},{6,12},{7,13},{8,14},{9,15},... | collective-permute-start | bytes 589832 | tf_op jit(solution)/shard_map/ppermute | solution.py:28
  162.8 19.8 %collective-permute-start.21 = (bf16[3,4,8,1024]{3,2,1,0:T(8,128)(2,1)}, bf16[3,4,8,1024]{3,2,1,0:T(8,128)(2,1)}, u32[]{:S(2)}, u32[]{:S(2)}) collective-permute-start(bf16[3,4,8,1024]{3,2,1,0:T(8,128)(2,1)} %get-tuple-element.50), channel_id=1, source_target_pairs={{0,8},{1,9},{2,10},{3,11},{4,12},{5,13},{6,14},{7,15},{8,0},{9,1},... | collective-permute-start | bytes 589832 | tf_op jit(solution)/shard_map/ppermute | solution.py:28
  164.4 23.4 %collective-permute-start.25 = (bf16[3,4,8,1024]{3,2,1,0:T(8,128)(2,1)}, bf16[3,4,8,1024]{3,2,1,0:T(8,128)(2,1)}, u32[]{:S(2)}, u32[]{:S(2)}) collective-permute-start(bf16[3,4,8,1024]{3,2,1,0:T(8,128)(2,1)} %get-tuple-element.54), channel_id=1, source_target_pairs={{0,10},{1,11},{2,12},{3,13},{4,14},{5,15},{6,0},{7,1},{8,2},{9,3},... | collective-permute-start | bytes 589832 | tf_op jit(solution)/shard_map/ppermute | solution.py:28
  166.3 28.9 %collective-permute-start.29 = (bf16[3,4,8,1024]{3,2,1,0:T(8,128)(2,1)S(1)}, bf16[3,4,8,1024]{3,2,1,0:T(8,128)(2,1)}, u32[]{:S(2)}, u32[]{:S(2)}) collective-permute-start(bf16[3,4,8,1024]{3,2,1,0:T(8,128)(2,1)S(1)} %copy-done.20), channel_id=1, source_target_pairs={{0,12},{1,13},{2,14},{3,15},{4,0},{5,1},{6,2},{7,3},{8,4},{9,5},{1... | collective-permute-start | bytes 589832 | tf_op jit(solution)/shard_map/ppermute | solution.py:28
  169.6 30.9 %all-to-all-start.3 = ((bf16[4,3,8,8,1024]{4,3,1,2,0:T(8,128)(2,1)}), bf16[4,3,8,8,1024]{4,3,1,2,0:T(8,128)(2,1)S(1)}, u32[]{:S(2)}, u32[]{:S(2)}) async-start(bf16[4,3,8,8,1024]{4,3,1,2,0:T(8,128)(2,1)} %bitcast.450), calls=%async_computation.3 | async-start | bytes 3145728 | tf_op jit(solution)/shard_map/all_to_all | solution.py:36
  174.5 22.6 %collective-permute-start.33 = (bf16[3,4,8,1024]{3,2,1,0:T(8,128)(2,1)S(1)}, bf16[3,4,8,1024]{3,2,1,0:T(8,128)(2,1)S(1)}, u32[]{:S(2)}, u32[]{:S(2)}) collective-permute-start(bf16[3,4,8,1024]{3,2,1,0:T(8,128)(2,1)S(1)} %copy-done.19), channel_id=1, source_target_pairs={{0,14},{1,15},{2,0},{3,1},{4,2},{5,3},{6,4},{7,5},{8,6},{9,7},{10,... | collective-permute-start | bytes 589832 | tf_op jit(solution)/shard_map/ppermute | solution.py:28
  201.6 25.4 %all-to-all-start = ((bf16[4,8,3,8,1024]{4,3,2,1,0:T(8,128)(2,1)}), bf16[4,8,3,8,1024]{4,3,2,1,0:T(8,128)(2,1)S(1)}, u32[]{:S(2)}, u32[]{:S(2)}) async-start(bf16[4,8,3,8,1024]{4,3,2,1,0:T(8,128)(2,1)} %copy.179), calls=%async_computation | async-start | bytes 3145728 | tf_op jit(solution)/shard_map/all_to_all | solution.py:36
  208.6 13.0 %collective-permute-start.10 = (bf16[4,3,8,1024]{3,2,1,0:T(8,128)(2,1)S(1)}, bf16[4,3,8,1024]{3,2,1,0:T(8,128)(2,1)S(1)}, u32[]{:S(2)}, u32[]{:S(2)}) collective-permute-start(bf16[4,3,8,1024]{3,2,1,0:T(8,128)(2,1)S(1)} %get-tuple-element.39), channel_id=1, source_target_pairs={{0,2},{1,3},{2,4},{3,5},{4,6},{5,7},{6,8},{7,9},{8,10},{9,11},{10,... | collective-permute-start | bytes 589832 | tf_op jit(solution)/shard_map/ppermute | solution.py:28
  209.2 21.4 %collective-permute-start.14 = (bf16[4,3,8,1024]{3,2,1,0:T(8,128)(2,1)}, bf16[4,3,8,1024]{3,2,1,0:T(8,128)(2,1)}, u32[]{:S(2)}, u32[]{:S(2)}) collective-permute-start(bf16[4,3,8,1024]{3,2,1,0:T(8,128)(2,1)} %get-tuple-element.43), channel_id=1, source_target_pairs={{0,4},{1,5},{2,6},{3,7},{4,8},{5,9},{6,10},{7,11},{8,12},{9,13},{1... | collective-permute-start | bytes 589832 | tf_op jit(solution)/shard_map/ppermute | solution.py:28
  212.4 24.3 %collective-permute-start.18 = (bf16[4,3,8,1024]{3,2,1,0:T(8,128)(2,1)}, bf16[4,3,8,1024]{3,2,1,0:T(8,128)(2,1)S(1)}, u32[]{:S(2)}, u32[]{:S(2)}) collective-permute-start(bf16[4,3,8,1024]{3,2,1,0:T(8,128)(2,1)} %get-tuple-element.47), channel_id=1, source_target_pairs={{0,6},{1,7},{2,8},{3,9},{4,10},{5,11},{6,12},{7,13},{8,14},{9,15},... | collective-permute-start | bytes 589832 | tf_op jit(solution)/shard_map/ppermute | solution.py:28
  213.0 29.4 %collective-permute-start.22 = (bf16[4,3,8,1024]{3,2,1,0:T(8,128)(2,1)}, bf16[4,3,8,1024]{3,2,1,0:T(8,128)(2,1)S(1)}, u32[]{:S(2)}, u32[]{:S(2)}) collective-permute-start(bf16[4,3,8,1024]{3,2,1,0:T(8,128)(2,1)} %get-tuple-element.51), channel_id=1, source_target_pairs={{0,8},{1,9},{2,10},{3,11},{4,12},{5,13},{6,14},{7,15},{8,0},{9,1},... | collective-permute-start | bytes 589832 | tf_op jit(solution)/shard_map/ppermute | solution.py:28
  218.3 26.9 %collective-permute-start.26 = (bf16[4,3,8,1024]{3,2,1,0:T(8,128)(2,1)}, bf16[4,3,8,1024]{3,2,1,0:T(8,128)(2,1)}, u32[]{:S(2)}, u32[]{:S(2)}) collective-permute-start(bf16[4,3,8,1024]{3,2,1,0:T(8,128)(2,1)} %get-tuple-element.55), channel_id=1, source_target_pairs={{0,10},{1,11},{2,12},{3,13},{4,14},{5,15},{6,0},{7,1},{8,2},{9,3},... | collective-permute-start | bytes 589832 | tf_op jit(solution)/shard_map/ppermute | solution.py:28
  221.7 30.7 %collective-permute-start.30 = (bf16[4,3,8,1024]{3,2,1,0:T(8,128)(2,1)}, bf16[4,3,8,1024]{3,2,1,0:T(8,128)(2,1)}, u32[]{:S(2)}, u32[]{:S(2)}) collective-permute-start(bf16[4,3,8,1024]{3,2,1,0:T(8,128)(2,1)} %get-tuple-element.59), channel_id=1, source_target_pairs={{0,12},{1,13},{2,14},{3,15},{4,0},{5,1},{6,2},{7,3},{8,4},{9,5},{1... | collective-permute-start | bytes 589832 | tf_op jit(solution)/shard_map/ppermute | solution.py:28
  227.1 38.6 %all-to-all-start.4 = ((bf16[4,8,3,8,1024]{4,3,2,1,0:T(8,128)(2,1)}), bf16[4,8,3,8,1024]{4,3,2,1,0:T(8,128)(2,1)S(1)}, u32[]{:S(2)}, u32[]{:S(2)}) async-start(bf16[4,8,3,8,1024]{4,3,2,1,0:T(8,128)(2,1)} %copy.225), calls=%async_computation.4 | async-start | bytes 3145728 | tf_op jit(solution)/shard_map/all_to_all | solution.py:36
  230.6 22.5 %collective-permute-start.34 = (bf16[4,3,8,1024]{3,2,1,0:T(8,128)(2,1)}, bf16[4,3,8,1024]{3,2,1,0:T(8,128)(2,1)S(1)}, u32[]{:S(2)}, u32[]{:S(2)}) collective-permute-start(bf16[4,3,8,1024]{3,2,1,0:T(8,128)(2,1)} %get-tuple-element.63), channel_id=1, source_target_pairs={{0,14},{1,15},{2,0},{3,1},{4,2},{5,3},{6,4},{7,5},{8,6},{9,7},{10,... | collective-permute-start | bytes 589832 | tf_op jit(solution)/shard_map/ppermute | solution.py:28
  236.7 29.9 %collective-permute-start.11 = (bf16[4,3,8,1024]{3,2,1,0:T(8,128)(2,1)}, bf16[4,3,8,1024]{3,2,1,0:T(8,128)(2,1)}, u32[]{:S(2)}, u32[]{:S(2)}) collective-permute-start(bf16[4,3,8,1024]{3,2,1,0:T(8,128)(2,1)} %get-tuple-element.40), channel_id=1, source_target_pairs={{0,2},{1,3},{2,4},{3,5},{4,6},{5,7},{6,8},{7,9},{8,10},{9,11},{10,... | collective-permute-start | bytes 589832 | tf_op jit(solution)/shard_map/ppermute | solution.py:28
  242.4 25.6 %collective-permute-start.15 = (bf16[4,3,8,1024]{3,2,1,0:T(8,128)(2,1)}, bf16[4,3,8,1024]{3,2,1,0:T(8,128)(2,1)}, u32[]{:S(2)}, u32[]{:S(2)}) collective-permute-start(bf16[4,3,8,1024]{3,2,1,0:T(8,128)(2,1)} %get-tuple-element.44), channel_id=1, source_target_pairs={{0,4},{1,5},{2,6},{3,7},{4,8},{5,9},{6,10},{7,11},{8,12},{9,13},{1... | collective-permute-start | bytes 589832 | tf_op jit(solution)/shard_map/ppermute | solution.py:28
  245.1 26.3 %collective-permute-start.19 = (bf16[4,3,8,1024]{3,2,1,0:T(8,128)(2,1)}, bf16[4,3,8,1024]{3,2,1,0:T(8,128)(2,1)}, u32[]{:S(2)}, u32[]{:S(2)}) collective-permute-start(bf16[4,3,8,1024]{3,2,1,0:T(8,128)(2,1)} %get-tuple-element.48), channel_id=1, source_target_pairs={{0,6},{1,7},{2,8},{3,9},{4,10},{5,11},{6,12},{7,13},{8,14},{9,15},... | collective-permute-start | bytes 589832 | tf_op jit(solution)/shard_map/ppermute | solution.py:28
  252.4 27.6 %collective-permute-start.23 = (bf16[4,3,8,1024]{3,2,1,0:T(8,128)(2,1)}, bf16[4,3,8,1024]{3,2,1,0:T(8,128)(2,1)}, u32[]{:S(2)}, u32[]{:S(2)}) collective-permute-start(bf16[4,3,8,1024]{3,2,1,0:T(8,128)(2,1)} %get-tuple-element.52), channel_id=1, source_target_pairs={{0,8},{1,9},{2,10},{3,11},{4,12},{5,13},{6,14},{7,15},{8,0},{9,1},... | collective-permute-start | bytes 589832 | tf_op jit(solution)/shard_map/ppermute | solution.py:28
  253.2 28.9 %collective-permute-start.27 = (bf16[4,3,8,1024]{3,2,1,0:T(8,128)(2,1)}, bf16[4,3,8,1024]{3,2,1,0:T(8,128)(2,1)}, u32[]{:S(2)}, u32[]{:S(2)}) collective-permute-start(bf16[4,3,8,1024]{3,2,1,0:T(8,128)(2,1)} %get-tuple-element.56), channel_id=1, source_target_pairs={{0,10},{1,11},{2,12},{3,13},{4,14},{5,15},{6,0},{7,1},{8,2},{9,3},... | collective-permute-start | bytes 589832 | tf_op jit(solution)/shard_map/ppermute | solution.py:28
  266.5 22.6 %collective-permute-start.37 = (bf16[96,8,1024]{2,0,1:T(8,128)(2,1)S(1)}, bf16[96,8,1024]{2,0,1:T(8,128)(2,1)S(1)}, u32[]{:S(2)}, u32[]{:S(2)}) collective-permute-start(bf16[96,8,1024]{2,0,1:T(8,128)(2,1)S(1)} %copy.226), channel_id=1, source_target_pairs={{0,1},{1,0},{2,3},{3,2},{4,5},{5,4},{6,7},{7,6},{8,9},{9,8},{10,11... | collective-permute-start | bytes 4718600 | tf_op jit(solution)/shard_map/ppermute | solution.py:32
  268.0 22.5 %collective-permute-start.7 = (bf16[96,8,1024]{2,0,1:T(8,128)(2,1)S(1)}, bf16[96,8,1024]{2,0,1:T(8,128)(2,1)S(1)}, u32[]{:S(2)}, u32[]{:S(2)}) collective-permute-start(bf16[96,8,1024]{2,0,1:T(8,128)(2,1)S(1)} %copy-done.11), channel_id=1, source_target_pairs={{0,1},{1,0},{2,3},{3,2},{4,5},{5,4},{6,7},{7,6},{8,9},{9,8},{10,11... | collective-permute-start | bytes 4718600 | tf_op jit(solution)/shard_map/ppermute | solution.py:32
  270.0 20.5 %copy-start.12 = (bf16[1,96,8,1024]{3,1,0,2:T(8,128)(2,1)}, bf16[1,96,8,1024]{3,1,0,2:T(8,128)(2,1)S(1)}, u32[]{:S(2)}) copy-start(bf16[1,96,8,1024]{3,1,0,2:T(8,128)(2,1)S(1)} %copy.227) | copy-start | bytes 4718596
  271.4 15.6 %collective-permute-start.31 = (bf16[4,3,8,1024]{3,2,1,0:T(8,128)(2,1)S(1)}, bf16[4,3,8,1024]{3,2,1,0:T(8,128)(2,1)S(1)}, u32[]{:S(2)}, u32[]{:S(2)}) collective-permute-start(bf16[4,3,8,1024]{3,2,1,0:T(8,128)(2,1)S(1)} %copy-done.22), channel_id=1, source_target_pairs={{0,12},{1,13},{2,14},{3,15},{4,0},{5,1},{6,2},{7,3},{8,4},{9,5},{1... | collective-permute-start | bytes 589832 | tf_op jit(solution)/shard_map/ppermute | solution.py:28
  280.0 9.1 %collective-permute-start.35 = (bf16[4,3,8,1024]{3,2,1,0:T(8,128)(2,1)S(1)}, bf16[4,3,8,1024]{3,2,1,0:T(8,128)(2,1)S(1)}, u32[]{:S(2)}, u32[]{:S(2)}) collective-permute-start(bf16[4,3,8,1024]{3,2,1,0:T(8,128)(2,1)S(1)} %copy-done.21), channel_id=1, source_target_pairs={{0,14},{1,15},{2,0},{3,1},{4,2},{5,3},{6,4},{7,5},{8,6},{9,7},{10,... | collective-permute-start | bytes 589832 | tf_op jit(solution)/shard_map/ppermute | solution.py:28
  294.8 11.4 %collective-permute-start.51 = (f32[4,96,2,96]{3,1,2,0:T(8,128)}, f32[4,96,2,96]{3,1,2,0:T(8,128)}, u32[]{:S(2)}, u32[]{:S(2)}) collective-permute-start(f32[4,96,2,96]{3,1,2,0:T(8,128)} %get-tuple-element.121), channel_id=1, source_target_pairs={{0,1},{1,0},{2,3},{3,2},{4,5},{5,4},{6,7},{7,6},{8,9},{9,8},{10,11... | collective-permute-start | bytes 884744 | tf_op jit(solution)/shard_map/ppermute | solution.py:32
  297.7 125.1 %all-to-all-start.1 = ((bf16[4,8,3,8,1024]{4,3,2,1,0:T(8,128)(2,1)}), bf16[4,8,3,8,1024]{4,3,2,1,0:T(8,128)(2,1)S(1)}, u32[]{:S(2)}, u32[]{:S(2)}) async-start(bf16[4,8,3,8,1024]{4,3,2,1,0:T(8,128)(2,1)} %bitcast.34), calls=%async_computation.1 | async-start | bytes 3145728 | tf_op jit(solution)/shard_map/all_to_all | solution.py:36
  422.8 111.0 %all-to-all-start.5 = ((bf16[4,8,3,8,1024]{4,3,2,1,0:T(8,128)(2,1)}), bf16[4,8,3,8,1024]{4,3,2,1,0:T(8,128)(2,1)S(1)}, u32[]{:S(2)}, u32[]{:S(2)}) async-start(bf16[4,8,3,8,1024]{4,3,2,1,0:T(8,128)(2,1)} %bitcast.109), calls=%async_computation.5 | async-start | bytes 3145728 | tf_op jit(solution)/shard_map/all_to_all | solution.py:36
  427.6 200.4 %all-reduce.2.cloned.1.call-start = ((), (), s32[]{:S(2)}) async-start(), calls=%async_computation.6 | async-start | bytes 1572864 | tf_op jit(solution)/shard_map/psum | solution.py:144
  521.7 12.5 %collective-permute-start.12 = (bf16[4,3,8,1024]{3,2,1,0:T(8,128)(2,1)}, bf16[4,3,8,1024]{3,2,1,0:T(8,128)(2,1)S(1)}, u32[]{:S(2)}, u32[]{:S(2)}) collective-permute-start(bf16[4,3,8,1024]{3,2,1,0:T(8,128)(2,1)} %get-tuple-element.41), channel_id=1, source_target_pairs={{0,2},{1,3},{2,4},{3,5},{4,6},{5,7},{6,8},{7,9},{8,10},{9,11},{10,... | collective-permute-start | bytes 589832 | tf_op jit(solution)/shard_map/ppermute | solution.py:28
  522.7 19.3 %collective-permute-start.16 = (bf16[4,3,8,1024]{3,2,1,0:T(8,128)(2,1)}, bf16[4,3,8,1024]{3,2,1,0:T(8,128)(2,1)S(1)}, u32[]{:S(2)}, u32[]{:S(2)}) collective-permute-start(bf16[4,3,8,1024]{3,2,1,0:T(8,128)(2,1)} %get-tuple-element.45), channel_id=1, source_target_pairs={{0,4},{1,5},{2,6},{3,7},{4,8},{5,9},{6,10},{7,11},{8,12},{9,13},{1... | collective-permute-start | bytes 589832 | tf_op jit(solution)/shard_map/ppermute | solution.py:28
  525.2 27.7 %collective-permute-start.20 = (bf16[4,3,8,1024]{3,2,1,0:T(8,128)(2,1)}, bf16[4,3,8,1024]{3,2,1,0:T(8,128)(2,1)}, u32[]{:S(2)}, u32[]{:S(2)}) collective-permute-start(bf16[4,3,8,1024]{3,2,1,0:T(8,128)(2,1)} %get-tuple-element.49), channel_id=1, source_target_pairs={{0,6},{1,7},{2,8},{3,9},{4,10},{5,11},{6,12},{7,13},{8,14},{9,15},... | collective-permute-start | bytes 589832 | tf_op jit(solution)/shard_map/ppermute | solution.py:28
  526.9 34.2 %collective-permute-start.24 = (bf16[4,3,8,1024]{3,2,1,0:T(8,128)(2,1)}, bf16[4,3,8,1024]{3,2,1,0:T(8,128)(2,1)}, u32[]{:S(2)}, u32[]{:S(2)}) collective-permute-start(bf16[4,3,8,1024]{3,2,1,0:T(8,128)(2,1)} %get-tuple-element.53), channel_id=1, source_target_pairs={{0,8},{1,9},{2,10},{3,11},{4,12},{5,13},{6,14},{7,15},{8,0},{9,1},... | collective-permute-start | bytes 589832 | tf_op jit(solution)/shard_map/ppermute | solution.py:28
  529.3 32.8 %collective-permute-start.28 = (bf16[4,3,8,1024]{3,2,1,0:T(8,128)(2,1)}, bf16[4,3,8,1024]{3,2,1,0:T(8,128)(2,1)}, u32[]{:S(2)}, u32[]{:S(2)}) collective-permute-start(bf16[4,3,8,1024]{3,2,1,0:T(8,128)(2,1)} %get-tuple-element.57), channel_id=1, source_target_pairs={{0,10},{1,11},{2,12},{3,13},{4,14},{5,15},{6,0},{7,1},{8,2},{9,3},... | collective-permute-start | bytes 589832 | tf_op jit(solution)/shard_map/ppermute | solution.py:28
  534.9 39.2 %collective-permute-start.32 = (bf16[4,3,8,1024]{3,2,1,0:T(8,128)(2,1)S(1)}, bf16[4,3,8,1024]{3,2,1,0:T(8,128)(2,1)S(1)}, u32[]{:S(2)}, u32[]{:S(2)}) collective-permute-start(bf16[4,3,8,1024]{3,2,1,0:T(8,128)(2,1)S(1)} %copy-done.24), channel_id=1, source_target_pairs={{0,12},{1,13},{2,14},{3,15},{4,0},{5,1},{6,2},{7,3},{8,4},{9,5},{1... | collective-permute-start | bytes 589832 | tf_op jit(solution)/shard_map/ppermute | solution.py:28
  542.1 35.0 %collective-permute-start.36 = (bf16[4,3,8,1024]{3,2,1,0:T(8,128)(2,1)S(1)}, bf16[4,3,8,1024]{3,2,1,0:T(8,128)(2,1)S(1)}, u32[]{:S(2)}, u32[]{:S(2)}) collective-permute-start(bf16[4,3,8,1024]{3,2,1,0:T(8,128)(2,1)S(1)} %copy-done.23), channel_id=1, source_target_pairs={{0,14},{1,15},{2,0},{3,1},{4,2},{5,3},{6,4},{7,5},{8,6},{9,7},{10,... | collective-permute-start | bytes 589832 | tf_op jit(solution)/shard_map/ppermute | solution.py:28
  552.9 28.1 %collective-permute-start.38 = (bf16[4,3,8,1024]{3,2,1,0:T(8,128)(2,1)S(1)}, bf16[4,3,8,1024]{3,2,1,0:T(8,128)(2,1)S(1)}, u32[]{:S(2)}, u32[]{:S(2)}) collective-permute-start(bf16[4,3,8,1024]{3,2,1,0:T(8,128)(2,1)S(1)} %get-tuple-element.66), channel_id=1, source_target_pairs={{0,2},{1,3},{2,4},{3,5},{4,6},{5,7},{6,8},{7,9},{8,10},{9,11},{10,... | collective-permute-start | bytes 589832 | tf_op jit(solution)/shard_map/ppermute | solution.py:28
  561.1 24.1 %collective-permute-start.39 = (bf16[4,3,8,1024]{3,2,1,0:T(8,128)(2,1)S(1)}, bf16[4,3,8,1024]{3,2,1,0:T(8,128)(2,1)S(1)}, u32[]{:S(2)}, u32[]{:S(2)}) collective-permute-start(bf16[4,3,8,1024]{3,2,1,0:T(8,128)(2,1)S(1)} %get-tuple-element.67), channel_id=1, source_target_pairs={{0,4},{1,5},{2,6},{3,7},{4,8},{5,9},{6,10},{7,11},{8,12},{9,13},{1... | collective-permute-start | bytes 589832 | tf_op jit(solution)/shard_map/ppermute | solution.py:28
  562.1 23.4 %collective-permute-start.40 = (bf16[4,3,8,1024]{3,2,1,0:T(8,128)(2,1)S(1)}, bf16[4,3,8,1024]{3,2,1,0:T(8,128)(2,1)S(1)}, u32[]{:S(2)}, u32[]{:S(2)}) collective-permute-start(bf16[4,3,8,1024]{3,2,1,0:T(8,128)(2,1)S(1)} %get-tuple-element.68), channel_id=1, source_target_pairs={{0,6},{1,7},{2,8},{3,9},{4,10},{5,11},{6,12},{7,13},{8,14},{9,15},... | collective-permute-start | bytes 589832 | tf_op jit(solution)/shard_map/ppermute | solution.py:28
  574.1 15.3 %collective-permute-start.41 = (bf16[4,3,8,1024]{3,2,1,0:T(8,128)(2,1)S(1)}, bf16[4,3,8,1024]{3,2,1,0:T(8,128)(2,1)S(1)}, u32[]{:S(2)}, u32[]{:S(2)}) collective-permute-start(bf16[4,3,8,1024]{3,2,1,0:T(8,128)(2,1)S(1)} %get-tuple-element.69), channel_id=1, source_target_pairs={{0,8},{1,9},{2,10},{3,11},{4,12},{5,13},{6,14},{7,15},{8,0},{9,1},... | collective-permute-start | bytes 589832 | tf_op jit(solution)/shard_map/ppermute | solution.py:28
  577.1 20.0 %collective-permute-start.42 = (bf16[4,3,8,1024]{3,2,1,0:T(8,128)(2,1)S(1)}, bf16[4,3,8,1024]{3,2,1,0:T(8,128)(2,1)S(1)}, u32[]{:S(2)}, u32[]{:S(2)}) collective-permute-start(bf16[4,3,8,1024]{3,2,1,0:T(8,128)(2,1)S(1)} %get-tuple-element.70), channel_id=1, source_target_pairs={{0,10},{1,11},{2,12},{3,13},{4,14},{5,15},{6,0},{7,1},{8,2},{9,3},... | collective-permute-start | bytes 589832 | tf_op jit(solution)/shard_map/ppermute | solution.py:28
  581.0 20.9 %collective-permute-start.43 = (bf16[4,3,8,1024]{3,2,1,0:T(8,128)(2,1)S(1)}, bf16[4,3,8,1024]{3,2,1,0:T(8,128)(2,1)S(1)}, u32[]{:S(2)}, u32[]{:S(2)}) collective-permute-start(bf16[4,3,8,1024]{3,2,1,0:T(8,128)(2,1)S(1)} %get-tuple-element.71), channel_id=1, source_target_pairs={{0,12},{1,13},{2,14},{3,15},{4,0},{5,1},{6,2},{7,3},{8,4},{9,5},{1... | collective-permute-start | bytes 589832 | tf_op jit(solution)/shard_map/ppermute | solution.py:28
  585.2 19.0 %collective-permute-start.44 = (bf16[4,3,8,1024]{3,2,1,0:T(8,128)(2,1)S(1)}, bf16[4,3,8,1024]{3,2,1,0:T(8,128)(2,1)S(1)}, u32[]{:S(2)}, u32[]{:S(2)}) collective-permute-start(bf16[4,3,8,1024]{3,2,1,0:T(8,128)(2,1)S(1)} %get-tuple-element.72), channel_id=1, source_target_pairs={{0,14},{1,15},{2,0},{3,1},{4,2},{5,3},{6,4},{7,5},{8,6},{9,7},{10,... | collective-permute-start | bytes 589832 | tf_op jit(solution)/shard_map/ppermute | solution.py:28
  608.4 8.2 %collective-permute-start.45 = (bf16[192,256]{1,0:T(8,128)(2,1)S(1)}, bf16[192,256]{1,0:T(8,128)(2,1)S(1)}, u32[]{:S(2)}, u32[]{:S(2)}) collective-permute-start(bf16[192,256]{1,0:T(8,128)(2,1)S(1)} %get-tuple-element.122), channel_id=1, source_target_pairs={{0,64},{64,128},{128,192},{192,0},{1,65},{65,129},{129,193},{193,1... | collective-permute-start | bytes 294920 | tf_op jit(solution)/shard_map/ppermute | solution.py:58
  610.1 6.5 %collective-permute-start.47 = (bf16[192,256]{1,0:T(8,128)(2,1)S(1)}, bf16[192,256]{1,0:T(8,128)(2,1)S(1)}, u32[]{:S(2)}, u32[]{:S(2)}) collective-permute-start(bf16[192,256]{1,0:T(8,128)(2,1)S(1)} %get-tuple-element.123), channel_id=1, source_target_pairs={{0,192},{64,0},{128,64},{192,128},{1,193},{65,1},{129,65},{193,129... | collective-permute-start | bytes 294920 | tf_op jit(solution)/shard_map/ppermute | solution.py:58
  612.5 6.1 collective-permute-start.46
  618.7 9.2 %collective-permute-start.50 = (bf16[192,256]{1,0:T(8,128)(2,1)S(1)}, bf16[192,256]{1,0:T(8,128)(2,1)S(1)}, u32[]{:S(2)}, u32[]{:S(2)}) collective-permute-start(bf16[192,256]{1,0:T(8,128)(2,1)S(1)} %fusion.39), channel_id=1, source_target_pairs={{0,192},{64,0},{128,64},{192,128},{1,193},{65,1},{129,65},{193,129... | collective-permute-start | bytes 294920 | tf_op jit(solution)/shard_map/ppermute | solution.py:63
  620.7 7.2 %collective-permute-start.49 = (bf16[192,256]{1,0:T(8,128)(2,1)S(1)}, bf16[192,256]{1,0:T(8,128)(2,1)S(1)}, u32[]{:S(2)}, u32[]{:S(2)}) collective-permute-start(bf16[192,256]{1,0:T(8,128)(2,1)S(1)} %fusion.39), channel_id=1, source_target_pairs={{0,128},{64,192},{128,0},{192,64},{1,129},{65,193},{129,1},{193,65... | collective-permute-start | bytes 294920 | tf_op jit(solution)/shard_map/ppermute | solution.py:63
  621.2 6.7 %collective-permute-start.48 = (bf16[192,256]{1,0:T(8,128)(2,1)S(1)}, bf16[192,256]{1,0:T(8,128)(2,1)S(1)}, u32[]{:S(2)}, u32[]{:S(2)}) collective-permute-start(bf16[192,256]{1,0:T(8,128)(2,1)S(1)} %fusion.39), channel_id=1, source_target_pairs={{0,64},{64,128},{128,192},{192,0},{1,65},{65,129},{129,193},{193,1... | collective-permute-start | bytes 294920 | tf_op jit(solution)/shard_map/ppermute | solution.py:63
  (22 other events, 77.8 us)
Sparse Core Ops, SparseCore 0:
  520.8 49.7 all-reduce.1

commit v2 on v0

v2 whole, which is shorter than its diff:
```python
import jax
import jax.numpy as jnp
from jax import lax
from jax.experimental import pallas as pl
from jax.experimental.pallas import tpu as pltpu
from jax.sharding import PartitionSpec as P

X, Z, C, Y = 4, 8, 2, 4
F32, BF16 = jnp.float32, jnp.bfloat16
VMEM_BYTES = 56 * 2**20


def spot(x, z, c):
    return ((x % X) * Z + z % Z) * C + c % C


def moved(dx, dz, dc):
    return [
        (spot(x, z, c), spot(x + dx, z + dz, c + dc))
        for x in range(X)
        for z in range(Z)
        for c in range(C)
    ]


CHIPS = [[spot(x, z, c) for x in range(X) for z in range(Z)] for c in range(C)]


def hop(array, dx=0, dz=0, dc=0):
    return lax.ppermute(array, "seq", moved(dx, dz, dc))


def everywhere(array):
    return lax.all_to_all(array, "seq", 0, 0, axis_index_groups=CHIPS, tiled=True)


def params():
    return pltpu.CompilerParams(vmem_limit_bytes=VMEM_BYTES)


def cost(flops, moved_bytes):
    return pl.CostEstimate(flops=flops, bytes_accessed=moved_bytes, transcendentals=0)


def gate_kernel(gates_ref, grad_ref, out_ref):
    width = gates_ref.shape[-1]
    for n in range(gates_ref.shape[0]):
        p = gates_ref[n, 0].astype(F32) * grad_ref[n, 0].astype(F32)
        out_ref[:, :, 0, :, n * width : (n + 1) * width] = p.astype(BF16)


def gate(gates, grad_out):
    count, A3, _, _, C8, width = gates.shape
    spec = pl.BlockSpec((count, 1, X, Z, C8, width), lambda a: (0, a, 0, 0, 0, 0))
    return pl.pallas_call(
        gate_kernel,
        grid=(A3,),
        in_specs=[spec, spec],
        out_specs=pl.BlockSpec((X, Z, 1, C8, count * width), lambda a: (0, 0, a, 0, 0)),
        out_shape=jax.ShapeDtypeStruct((X, Z, A3, C8, count * width), BF16),
        compiler_params=params(),
        cost_estimate=cost(gates.size, 6 * gates.size),
        name="gate",
    )(gates, grad_out)


def mix_kernel(weights_ref, inputs_ref, out_ref):
    width = inputs_ref.shape[-1]
    for n in range(inputs_ref.shape[0]):
        mixed = jnp.dot(weights_ref[0], inputs_ref[n, 0], preferred_element_type=F32)
        mixed = mixed.astype(BF16).reshape(X, Z, -1, width)
        out_ref[:, :, 0, :, n * width : (n + 1) * width] = mixed


def mix(weights, inputs):
    count, A3, B, width = inputs.shape
    C8 = B // (X * Z)
    return pl.pallas_call(
        mix_kernel,
        grid=(A3,),
        in_specs=[
            pl.BlockSpec((1, B, B), lambda a: (a, 0, 0)),
            pl.BlockSpec((count, 1, B, width), lambda a: (0, a, 0, 0)),
        ],
        out_specs=pl.BlockSpec((X, Z, 1, C8, count * width), lambda a: (0, 0, a, 0, 0)),
        out_shape=jax.ShapeDtypeStruct((X, Z, A3, C8, count * width), BF16),
        compiler_params=params(),
        cost_estimate=cost(2 * inputs.size * B, 4 * inputs.size),
        name="mix",
    )(weights, inputs)


def inner_kernel(own_m_ref, other_m_ref, own_ref, other_ref, out_ref):
    total = jnp.dot(own_m_ref[...], own_ref[...], preferred_element_type=F32)
    total += jnp.dot(other_m_ref[...], other_ref[...], preferred_element_type=F32)
    out_ref[...] = total.astype(BF16)


def inner_product(own_m, other_m, own, other):
    rows, width = own.shape
    tile = 256
    whole = pl.BlockSpec((rows, rows), lambda i: (0, 0))
    part = pl.BlockSpec((rows, tile), lambda i: (0, i))
    return pl.pallas_call(
        inner_kernel,
        grid=(width // tile,),
        in_specs=[whole, whole, part, part],
        out_specs=part,
        out_shape=jax.ShapeDtypeStruct((rows, width), BF16),
        compiler_params=params(),
        cost_estimate=cost(4 * rows * rows * width, 6 * rows * width),
        name="inner",
    )(own_m, other_m, own, other)


def first_kernel(y_ref, inputs_ref, inner_ref, own_ref, *refs):
    outs, held = refs[: Y - 1], refs[Y - 1]
    y = y_ref[0]
    rows, width = inputs_ref.shape[2:]
    total = None
    for n in range(inputs_ref.shape[0]):
        inner = inner_ref[:, 0, :, n * width : (n + 1) * width].reshape(rows, width)
        product = lax.dot_general(
            inputs_ref[n, 0], inner, (((1,), (1,)), ((), ())), preferred_element_type=F32
        )
        total = product if total is None else total + product
    held[...] = total.reshape(held.shape)
    own_ref[0] = held[y]
    for k, out in enumerate(outs):
        out[0] = held[lax.rem(y + k + 1, Y)].astype(BF16)


def first_gradient(y, inputs, inner):
    count, A3, B, width = inputs.shape
    rows = B // Y
    index = lambda a, y: (a, 0, 0)
    part = (A3, rows, B)
    return pl.pallas_call(
        first_kernel,
        grid_spec=pltpu.PrefetchScalarGridSpec(
            num_scalar_prefetch=1,
            grid=(A3,),
            in_specs=[
                pl.BlockSpec((count, 1, B, width), lambda a, y: (0, a, 0, 0)),
                pl.BlockSpec((X * Z, 1, B // (X * Z), count * width), lambda a, y: (0, a, 0, 0)),
            ],
            out_specs=[pl.BlockSpec((1, rows, B), index)] * Y,
            scratch_shapes=[pltpu.VMEM((Y, rows, B), F32)],
        ),
        out_shape=[jax.ShapeDtypeStruct(part, F32)] + [jax.ShapeDtypeStruct(part, BF16)] * (Y - 1),
        compiler_params=params(),
        cost_estimate=cost(2 * inputs.size * B, 4 * inputs.size),
        name="first",
    )(y, inputs, inner)


def result_kernel(weights_ref, inner_ref, out_ref):
    rows, width = out_ref.shape[2:]
    for n in range(out_ref.shape[0]):
        inner = inner_ref[:, 0, :, n * width : (n + 1) * width].reshape(rows, width)
        product = jnp.dot(weights_ref[0], inner, preferred_element_type=F32)
        out_ref[n, 0] = product.astype(BF16)


def result(weights, inner, shape):
    count, A3, B, width = shape
    return pl.pallas_call(
        result_kernel,
        grid=(A3,),
        in_specs=[
            pl.BlockSpec((1, B, B), lambda a: (a, 0, 0)),
            pl.BlockSpec((X * Z, 1, B // (X * Z), count * width), lambda a: (0, a, 0, 0)),
        ],
        out_specs=pl.BlockSpec((count, 1, B, width), lambda a: (0, a, 0, 0)),
        out_shape=jax.ShapeDtypeStruct(shape, BF16),
        compiler_params=params(),
        cost_estimate=cost(2 * inner.size * B, 4 * inner.size),
        name="result",
    )(weights, inner)


def dp_hop(array, k):
    return lax.ppermute(array, "dp", [(i, (i + k) % Y) for i in range(Y)])


def place_kernel(y_ref, *refs):
    parts, out = refs[:Y], refs[Y]
    y = y_ref[0]
    rows = parts[0].shape[1]
    for k in range(Y):
        at = pl.multiple_of(lax.rem(y + Y - k, Y) * rows, rows)
        out[:, pl.ds(at, rows), :] = parts[k][...].astype(F32)


def dp_sum(y, own, sent):
    got = [dp_hop(piece, k + 1) for k, piece in enumerate(sent)]
    for piece in got:
        own = own + piece.astype(F32)
    small = own.astype(BF16)
    parts = [own] + [dp_hop(small, k) for k in range(1, Y)]
    scalar = pl.BlockSpec(memory_space=pltpu.SMEM)
    whole = pl.BlockSpec(memory_space=pltpu.VMEM)
    a, b, c = own.shape
    return pl.pallas_call(
        place_kernel,
        in_specs=[scalar] + [whole] * Y,
        out_specs=whole,
        out_shape=jax.ShapeDtypeStruct((a, b * Y, c), F32),
        compiler_params=params(),
        cost_estimate=cost(own.size, 6 * own.size),
        name="place",
    )(y, *parts)


def shards(values, gates, grad_out, first_blocks, second_blocks):
    count, rows, width = values.shape
    A3, B = first_blocks.shape[:2]
    C8 = B // (X * Z)
    C4, A = second_blocks.shape[:2]
    half = A // C
    tall = half * C8
    lanes = count * width
    here = lax.axis_index("seq").astype(jnp.int32)
    core = here % C
    ys = lax.axis_index("dp").astype(jnp.int32).reshape(1)

    gates = gates.reshape(count, A3, X, Z, C8, width)
    grad_out = grad_out.reshape(count, A3, X, Z, C8, width)
    gated = gate(gates, grad_out)
    own = everywhere(gated.reshape(X * Z, A3 * C8, lanes)).reshape(tall, lanes)

    values, first_blocks, second_blocks, _ = lax.optimization_barrier(
        (values, first_blocks, second_blocks, gated)
    )
    inputs = values.reshape(count, A3, B, width)
    mixed = mix(first_blocks.transpose(0, 2, 1), inputs)
    mixed, _ = lax.optimization_barrier((mixed, own))
    cols_u = everywhere(mixed.reshape(X * Z, A3 * C8, lanes)).reshape(tall, lanes)

    second = second_blocks.reshape(C4, half // A3, C, A3, A)
    mine = lax.dynamic_index_in_dim(second, core, 2, keepdims=False)
    other = hop(lax.dynamic_index_in_dim(second, 1 - core, 2, keepdims=False), dc=1)
    pair = jnp.where(core == 0, jnp.stack([mine, other]), jnp.stack([other, mine]))
    pair = pair.reshape(C8, half, A).transpose(1, 0, 2).reshape(tall, A)
    e = lax.broadcasted_iota(jnp.int32, (A, tall), 0)
    q = lax.broadcasted_iota(jnp.int32, (A, tall), 1) // C8
    spread = [
        (e == (q // A3) * (C * A3) + ((core + r) % C) * A3 + q % A3).astype(BF16) for r in range(C)
    ]
    same = (
        lax.broadcasted_iota(jnp.int32, (tall, tall), 0) % C8
        == lax.broadcasted_iota(jnp.int32, (tall, tall), 1) % C8
    )
    wide = [
        jnp.where(same, jnp.dot(pair, s, preferred_element_type=F32), 0).astype(BF16)
        for s in spread
    ]

    cols_g = (own, hop(own, dc=1))
    inner = inner_product(*wide, *cols_g)
    inner, _ = lax.optimization_barrier((inner, cols_u))
    inner = everywhere(inner.reshape(X * Z, A3 * C8, lanes)).reshape(X * Z, A3, C8, lanes)

    grad_second = 0
    for r in range(C):
        product = lax.dot_general(
            cols_u, cols_g[r], (((1,), (1,)), ((), ())), preferred_element_type=F32
        )
        grad_second += lax.dot_general(
            jnp.where(same, product, 0),
            spread[r].astype(F32),
            (((1,), (1,)), ((), ())),
            precision=lax.Precision.HIGHEST,
            preferred_element_type=F32,
        )
    grad_second = grad_second.reshape(half, C, C4, A).transpose(1, 2, 0, 3)
    mine = lax.dynamic_index_in_dim(grad_second, core, 0, keepdims=False)
    other = hop(lax.dynamic_index_in_dim(grad_second, 1 - core, 0, keepdims=False), dc=1)
    mine, other = (g.reshape(C4, half // A3, 1, A3, A) for g in (mine, other))
    pair = jnp.where(
        core == 0, jnp.concatenate([mine, other], 2), jnp.concatenate([other, mine], 2)
    )
    pair = pair.reshape(C4, A, A)
    parts = [
        lax.dynamic_slice_in_dim(pair, (ys[0] + k) % Y * (A // Y), A // Y, 1) for k in range(Y)
    ]
    grad_second = dp_sum(ys, parts[0], [part.astype(BF16) for part in parts[1:]])

    inner, grad_second = lax.optimization_barrier((inner, grad_second))

    own, *sent = first_gradient(ys, inputs, inner)
    grad_values = result(first_blocks, inner, inputs.shape).reshape(count, rows, width)
    own, grad_values = lax.optimization_barrier((own, grad_values))
    grad_first = dp_sum(ys, own, sent)
    return grad_values, grad_first, grad_second


def solution(mesh):
    return jax.shard_map(
        shards,
        mesh=mesh,
        in_specs=(
            P("dp", "seq", None),
            P("dp", "seq", None),
            P("dp", "seq", None),
            P("seq", None, None),
            P("seq", None, None),
        ),
        out_specs=(P("dp", "seq", None), P("seq", None, None), P("seq", None, None)),
        check_vma=False,
    )
```

time: 343 us -> 282 us (0.82)
  waiting for transfers between devices: 238 us -> 160 us
  Pallas kernels: 0 us -> 35.5 us
  local copies, waits for them, and re-layouts: 41.1 us -> 14.6 us
  starting transfers between devices: 30 us -> 45.2 us
  between operations: 14.2 us -> 0.84 us
  matrix products: 12.7 us -> 18.3 us
    psum x1 -> x0, waiting for transfers between devices: 51.2 us -> none  [shards(): grad_first, grad_second = lax.psum((grad_first, grad_second), 'dp')]
    all_to_all x3, waiting for transfers between devices: 187 us -> 144 us  [everywhere(): lax.all_to_all(array, 'seq', 0, 0, axis_index_groups=CHIPS, tiled=True)]
    pallas_call x0 -> x7, Pallas kernels: none -> 35.5 us  [the longest x1 10.6 us: inner_product(): pl.pallas_call(inner_kernel, grid=(width // tile,), in_specs=[whole, whol...]
    ppermute x0 -> x15, starting transfers between devices: none -> 21 us  [the longest x12 20.4 us: dp_hop(): return lax.ppermute(array, 'dp', [(i, (i + k) % Y) for i in range(Y)])]
    all_to_all x5 -> x0, local copies, waits for them, and re-layouts: 18 us -> none  [the longest x3 11.6 us: shards(): lax.all_to_all(jnp.einsum('cae,necd->nacd', second_blocks, scaled_cols, p...]
    ppermute x0 -> x15, waiting for transfers between devices: none -> 16.1 us  [the longest x12 11.2 us: dp_hop(): return lax.ppermute(array, 'dp', [(i, (i + k) % Y) for i in range(Y)])]
    convert_element_type x3 -> x0, local copies, waits for them, and re-layouts: 12.2 us -> none  [the longest x1 4.96 us: shards(): inner = lax.all_to_all(jnp.einsum('cae,necd->nacd', second_blocks, scaled...]
    dot_general x5 -> x6, matrix products: 12.7 us -> 18.3 us  [the longest x2 10 us: shards(): lax.dot_general(cols_u, cols_g[r], (((1,), (1,)), ((), ())), preferred_el...]
  transfers between devices with their start and end apart: 4 -> 18, of which waited for: 4 -> 13; matrix products, arithmetic and copies ran while one was open for 8% -> 12% of each run, Pallas kernels for 0% -> 8%
where the time goes in v2:
time: 282 us; the launch traced here: 279 us
  waiting for transfers between devices  160 us (57%)
  starting transfers between devices  45.2 us (16%)
  Pallas kernels  35.5 us (13%)
  matrix products  18.3 us (6%)
  local copies, waits for them, and re-layouts  14.6 us (5%)
  other arithmetic  5.19 us (2%)
    all_to_all x3, waiting for transfers between devices, everywhere(): lax.all_to_all(array, 'seq', 0, 0, axis_index_groups=CHIPS, tiled=True)  144 us
    all_to_all x3, starting transfers between devices, everywhere(): lax.all_to_all(array, 'seq', 0, 0, axis_index_groups=CHIPS, tiled=True)  24.3 us
    ppermute x12, starting transfers between devices, dp_hop(): return lax.ppermute(array, 'dp', [(i, (i + k) % Y) for i in range(Y)])  20.4 us
    ppermute x12, waiting for transfers between devices, dp_hop(): return lax.ppermute(array, 'dp', [(i, (i + k) % Y) for i in range(Y)])  11.2 us
    pallas_call x1, Pallas kernels, inner_product(): pl.pallas_call(inner_kernel, grid=(width // tile,), in_specs=[whole, whol...  10.6 us
    dot_general x2, matrix products, shards(): lax.dot_general(cols_u, cols_g[r], (((1,), (1,)), ((), ())), preferred_el...  10 us
  transfers between devices with their start and end apart: 18, of which 13 were waited for; matrix products, arithmetic and copies ran while one was open for 12% of the time, Pallas kernels for 8%

profile of v2, /device:TPU:96, one launch (start us, length us, event | category | flops | bytes accessed | tf_op | source)
XLA Modules:
  0.0 279.4 jit_solution(15610158215776301189)
XLA Ops:
  0.6 5.4 %gate.1 = bf16[4,8,3,8,2048]{4,3,2,1,0:T(8,128)(2,1)} custom-call(bf16[2,3,4,8,8,1024]{5,4,3,2,1,0:T(8,128)(2,1)} %bitcast.51, bf16[2,3,4,8,8,1024]{5,4,3,2,1,0:T(8,128)(2,1)} %bitcast.52), custom_call_target="tpu_custom_call" | custom-call | flops 1572864 | bytes 9437184 | tf_op jit(solution)/shard_map/gate/pallas_call | solution.py:55
  6.0 10.4 %all-to-all-start = ((bf16[32,24,2048]{2,1,0:T(8,128)(2,1)}), bf16[32,24,2048]{2,1,0:T(8,128)(2,1)S(1)}, u32[]{:S(2)}, u32[]{:S(2)}) async-start(bf16[32,24,2048]{2,1,0:T(8,128)(2,1)} %bitcast.45), calls=%async_computation | async-start | bytes 6291456 | tf_op jit(solution)/shard_map/all_to_all | solution.py:34
  16.5 0.9 copy.12
  17.4 5.3 %mix.1 = bf16[4,8,3,8,2048]{4,3,2,1,0:T(8,128)(2,1)} custom-call(bf16[3,256,256]{2,1,0:T(8,128)(2,1)} %bitcast.56, bf16[2,3,256,1024]{3,2,1,0:T(8,128)(2,1)} %bitcast.42), custom_call_target="tpu_custom_call" | custom-call | flops 805306368 | bytes 6291456 | tf_op jit(solution)/shard_map/mix/pallas_call | solution.py:78
  22.7 67.4 %all-to-all-done = bf16[32,24,2048]{2,1,0:T(8,128)(2,1)S(1)} async-done(((bf16[32,24,2048]{2,1,0:T(8,128)(2,1)}), bf16[32,24,2048]{2,1,0:T(8,128)(2,1)S(1)}, u32[]{:S(2)}, u32[]{:S(2)}) %all-to-all-start) | async-done | bytes 3145760 | tf_op jit(solution)/shard_map/all_to_all | solution.py:34
  90.1 6.9 %all-to-all-start.1 = ((bf16[32,24,2048]{2,1,0:T(8,128)(2,1)}), bf16[32,24,2048]{2,1,0:T(8,128)(2,1)}, u32[]{:S(2)}, u32[]{:S(2)}) async-start(bf16[32,24,2048]{2,1,0:T(8,128)(2,1)} %bitcast.44), calls=%async_computation.1 | async-start | bytes 6291456 | tf_op jit(solution)/shard_map/all_to_all | solution.py:34
  97.0 0.1 collective-permute-start.1
  97.1 1.3 copy.11
  98.4 0.9 dynamic-slice_bitcast_fusion.2
  99.3 0.5 collective-permute-start
  99.8 0.6 fusion.33
  100.4 2.8 %collective-permute-done = bf16[4,32,3,192]{3,0,2,1:T(4,128)(2,1)S(1)} collective-permute-done((bf16[4,32,3,192]{3,0,2,1:T(4,128)(2,1)}, bf16[4,32,3,192]{3,0,2,1:T(4,128)(2,1)S(1)}, u32[]{:S(2)}, u32[]{:S(2)}) %collective-permute-start) | collective-permute-done | bytes 147488 | tf_op jit(solution)/shard_map/ppermute | solution.py:30
  103.2 0.7 copy-done.5
  103.9 1.7 maximum_select_fusion.1
  105.6 1.0 select_n.146
  106.6 2.6 select_convert_fusion.other_m_ref
  109.2 1.5 select_convert_fusion.1.own_m_ref
  110.7 10.6 %inner.1 = bf16[768,2048]{1,0:T(8,128)(2,1)} custom-call(bf16[768,768]{1,0:T(8,128)(2,1)} %select_convert_fusion.1.own_m_ref, bf16[768,768]{1,0:T(8,128)(2,1)} %select_convert_fusion.other_m_ref, bf16[768,2048]{1,0:T(8,128)(2,1)} %bitcast.48, bf16[768,2048]{1,0:T(8,128)(2,1)} %collective-permute-done.1.other_ref), custom_call_target="tpu_custom_call" | custom-call | flops 4831838208 | bytes 9437184 | tf_op jit(solution)/shard_map/inner/pallas_call | solution.py:104
  121.3 49.1 %all-to-all-done.1 = bf16[32,24,2048]{2,1,0:T(8,128)(2,1)} async-done(((bf16[32,24,2048]{2,1,0:T(8,128)(2,1)}), bf16[32,24,2048]{2,1,0:T(8,128)(2,1)}, u32[]{:S(2)}, u32[]{:S(2)}) %all-to-all-start.1) | async-done | bytes 3145760 | tf_op jit(solution)/shard_map/all_to_all | solution.py:34
  170.4 7.0 %all-to-all-start.2 = ((bf16[32,24,2048]{2,1,0:T(8,128)(2,1)}), bf16[32,24,2048]{2,1,0:T(8,128)(2,1)S(1)}, u32[]{:S(2)}, u32[]{:S(2)}) async-start(bf16[32,24,2048]{2,1,0:T(8,128)(2,1)} %bitcast.46), calls=%async_computation.2 | async-start | bytes 6291456 | tf_op jit(solution)/shard_map/all_to_all | solution.py:34
  177.4 5.5 %fusion.61 = f32[768,768]{1,0:T(8,128)S(1)} fusion(bf16[768,2048]{1,0:T(8,128)(2,1)} %bitcast.15, bf16[768,2048]{1,0:T(8,128)(2,1)} %collective-permute-done.1.other_ref), kind=kOutput, calls=%fused_computation.80 | convolution fusion | flops 2415919104 | bytes 8650752 | tf_op jit(solution)/shard_map/dot_general | solution.py:266
  182.9 0.0 copy-start.2
  182.9 1.7 fusion
  184.6 0.2 copy-done.2
  184.8 4.5 %fusion.60 = f32[768,768]{1,0:T(8,128)S(1)} fusion(bf16[768,2048]{1,0:T(8,128)(2,1)} %bitcast.15, bf16[768,2048]{1,0:T(8,128)(2,1)S(1)} %bitcast.49), kind=kOutput, calls=%fused_computation.79 | convolution fusion | flops 2415919104 | bytes 8650752 | tf_op jit(solution)/shard_map/dot_general | solution.py:266
  189.3 2.5 fusion.4
  191.9 2.2 copy.13
  194.1 2.2 reshape.78
  196.3 2.0 constant_dynamic-slice_fusion.4
  198.3 0.0 collective-permute-start.2
  198.3 2.1 collective-permute-done.2
  200.4 1.4 maximum_select_fusion
  201.8 0.1 copy.14
  201.9 0.1 constant_dynamic-slice_fusion.2
  202.0 1.7 collective-permute-start.3
  203.7 3.0 %collective-permute-start.4 = (bf16[4,48,192]{2,1,0:T(8,128)(2,1)S(1)}, bf16[4,48,192]{2,1,0:T(8,128)(2,1)S(1)}, u32[]{:S(2)}, u32[]{:S(2)}) collective-permute-start(bf16[4,48,192]{2,1,0:T(8,128)(2,1)S(1)} %copy.32), channel_id=1, source_target_pairs={{0,128},{64,192},{128,0},{192,64},{1,129},{65,193},{129,1},{193,65... | collective-permute-start | bytes 221192 | tf_op jit(solution)/shard_map/ppermute | solution.py:183
  206.7 1.4 collective-permute-start.5
  208.1 0.1 collective-permute-done.3
  208.2 3.3 %collective-permute-done.4 = bf16[4,48,192]{2,1,0:T(8,128)(2,1)S(1)} collective-permute-done((bf16[4,48,192]{2,1,0:T(8,128)(2,1)S(1)}, bf16[4,48,192]{2,1,0:T(8,128)(2,1)S(1)}, u32[]{:S(2)}, u32[]{:S(2)}) %collective-permute-start.4) | collective-permute-done | bytes 73760 | tf_op jit(solution)/shard_map/ppermute | solution.py:183
  211.5 0.0 collective-permute-done.5
  211.5 0.7 fusion.58
  212.2 1.4 collective-permute-start.6
  213.6 2.6 collective-permute-start.7
  216.1 1.4 collective-permute-start.8
  217.5 1.1 collective-permute-done.6.refs_1_
  218.7 1.1 collective-permute-done.7.refs_2_
  219.8 1.0 collective-permute-done.8.refs_3_
  220.8 0.6 copy-done.12
  221.4 2.0 place.2
  223.4 27.2 %all-to-all-done.2 = bf16[32,24,2048]{2,1,0:T(8,128)(2,1)S(1)} async-done(((bf16[32,24,2048]{2,1,0:T(8,128)(2,1)}), bf16[32,24,2048]{2,1,0:T(8,128)(2,1)S(1)}, u32[]{:S(2)}, u32[]{:S(2)}) %all-to-all-start.2) | async-done | bytes 3145760 | tf_op jit(solution)/shard_map/all_to_all | solution.py:34
  250.6 1.6 copy-done
  252.3 4.9 %first.1 = (f32[3,64,256]{2,1,0:T(8,128)}, bf16[3,64,256]{2,1,0:T(8,128)(2,1)}, bf16[3,64,256]{2,1,0:T(8,128)(2,1)}, bf16[3,64,256]{2,1,0:T(8,128)(2,1)}) custom-call(s32[1]{0:T(128)} %bitcast.y_ref, bf16[2,3,256,1024]{3,2,1,0:T(8,128)(2,1)} %bitcast.43, bf16[32,3,8,2048]{3,2,1,0:T(8,128)(2,1)} %bitcast.40), custom_call_target="tpu_custom_call" | custom-call | flops 805306368 | bytes 6291456 | tf_op jit(solution)/shard_map/first/pallas_call | solution.py:138
  257.2 3.3 %collective-permute-start.10 = (bf16[3,64,256]{2,1,0:T(8,128)(2,1)}, bf16[3,64,256]{2,1,0:T(8,128)(2,1)S(1)}, u32[]{:S(2)}, u32[]{:S(2)}) collective-permute-start(bf16[3,64,256]{2,1,0:T(8,128)(2,1)} %get-tuple-element.26), channel_id=1, source_target_pairs={{0,128},{64,192},{128,0},{192,64},{1,129},{65,193},{129,1},{193,65... | collective-permute-start | bytes 294920 | tf_op jit(solution)/shard_map/ppermute | solution.py:183
  260.4 1.1 collective-permute-start.11
  261.5 1.0 collective-permute-start.9
  262.5 5.2 %result.1 = bf16[2,3,256,1024]{3,2,1,0:T(8,128)(2,1)} custom-call(bf16[3,256,256]{2,1,0:T(8,128)(2,1)} %weights_ref, bf16[32,3,8,2048]{3,2,1,0:T(8,128)(2,1)} %bitcast.41), custom_call_target="tpu_custom_call" | custom-call | flops 805306368 | bytes 6291456 | tf_op jit(solution)/shard_map/result/pallas_call | solution.py:167
  267.7 0.7 fusion.57
  268.4 0.7 collective-permute-start.12
  269.1 3.1 %collective-permute-start.13 = (bf16[3,64,256]{2,1,0:T(8,128)(2,1)S(1)}, bf16[3,64,256]{2,1,0:T(8,128)(2,1)S(1)}, u32[]{:S(2)}, u32[]{:S(2)}) collective-permute-start(bf16[3,64,256]{2,1,0:T(8,128)(2,1)S(1)} %get-tuple-element.29), channel_id=1, source_target_pairs={{0,128},{64,192},{128,0},{192,64},{1,129},{65,193},{129,1},{193,65... | collective-permute-start | bytes 294920 | tf_op jit(solution)/shard_map/ppermute | solution.py:183
  272.2 2.3 collective-permute-done.12.refs_1_
  274.5 1.3 collective-permute-done.13.refs_2_
  275.8 1.0 collective-permute-done.14.refs_3_
  276.8 0.6 copy-done.11
  277.4 2.0 place.3
  (35 shorter events, 0.1 us)
Async XLA Ops:
  6.0 10.4 %copy-start.3 = (bf16[3,256,256]{2,1,0:T(8,128)(2,1)S(1)}, bf16[3,256,256]{2,1,0:T(8,128)(2,1)}, u32[]{:S(2)}) copy-start(bf16[3,256,256]{2,1,0:T(8,128)(2,1)} %weights_ref) | copy-start | bytes 1179652
  6.0 84.0 %all-to-all-start = ((bf16[32,24,2048]{2,1,0:T(8,128)(2,1)}), bf16[32,24,2048]{2,1,0:T(8,128)(2,1)S(1)}, u32[]{:S(2)}, u32[]{:S(2)}) async-start(bf16[32,24,2048]{2,1,0:T(8,128)(2,1)} %bitcast.45), calls=%async_computation | async-start | bytes 6291456 | tf_op jit(solution)/shard_map/all_to_all | solution.py:34
  90.1 6.9 %copy-start.1 = (bf16[32,24,2048]{2,1,0:T(8,128)(2,1)}, bf16[32,24,2048]{2,1,0:T(8,128)(2,1)S(1)}, u32[]{:S(2)}) copy-start(bf16[32,24,2048]{2,1,0:T(8,128)(2,1)S(1)} %all-to-all-done) | copy-start | bytes 9437188
  90.1 80.3 %all-to-all-start.1 = ((bf16[32,24,2048]{2,1,0:T(8,128)(2,1)}), bf16[32,24,2048]{2,1,0:T(8,128)(2,1)}, u32[]{:S(2)}, u32[]{:S(2)}) async-start(bf16[32,24,2048]{2,1,0:T(8,128)(2,1)} %bitcast.44), calls=%async_computation.1 | async-start | bytes 6291456 | tf_op jit(solution)/shard_map/all_to_all | solution.py:34
  97.0 13.7 %collective-permute-start.1 = (bf16[768,2048]{1,0:T(8,128)(2,1)S(1)}, bf16[768,2048]{1,0:T(8,128)(2,1)}, u32[]{:S(2)}, u32[]{:S(2)}) collective-permute-start(bf16[768,2048]{1,0:T(8,128)(2,1)S(1)} %bitcast.47), channel_id=1, source_target_pairs={{0,1},{1,0},{2,3},{3,2},{4,5},{5,4},{6,7},{7,6},{8,9},{9,8},{10,11... | collective-permute-start | bytes 9437192 | tf_op jit(solution)/shard_map/ppermute | solution.py:30
  99.3 3.9 %collective-permute-start = (bf16[4,32,3,192]{3,0,2,1:T(4,128)(2,1)}, bf16[4,32,3,192]{3,0,2,1:T(4,128)(2,1)S(1)}, u32[]{:S(2)}, u32[]{:S(2)}) collective-permute-start(bf16[4,32,3,192]{3,0,2,1:T(4,128)(2,1)} %get-tuple-element.39), channel_id=1, source_target_pairs={{0,1},{1,0},{2,3},{3,2},{4,5},{5,4},{6,7},{7,6},{8,9},{9,8},{10,11... | collective-permute-start | bytes 442376 | tf_op jit(solution)/shard_map/ppermute | solution.py:30
  103.2 0.7 copy-start.5
  106.6 2.6 copy-start.4
  106.6 2.6 copy-start.13
  106.6 2.6 copy-start.14
  170.4 80.2 %all-to-all-start.2 = ((bf16[32,24,2048]{2,1,0:T(8,128)(2,1)}), bf16[32,24,2048]{2,1,0:T(8,128)(2,1)S(1)}, u32[]{:S(2)}, u32[]{:S(2)}) async-start(bf16[32,24,2048]{2,1,0:T(8,128)(2,1)} %bitcast.46), calls=%async_computation.2 | async-start | bytes 6291456 | tf_op jit(solution)/shard_map/all_to_all | solution.py:34
  182.9 1.9 copy-start.2
  198.3 2.1 collective-permute-start.2
  202.0 6.2 %collective-permute-start.3 = (bf16[4,48,192]{2,1,0:T(8,128)(2,1)S(1)}, bf16[4,48,192]{2,1,0:T(8,128)(2,1)S(1)}, u32[]{:S(2)}, u32[]{:S(2)}) collective-permute-start(bf16[4,48,192]{2,1,0:T(8,128)(2,1)S(1)} %copy.33), channel_id=1, source_target_pairs={{0,64},{64,128},{128,192},{192,0},{1,65},{65,129},{129,193},{193,1... | collective-permute-start | bytes 221192 | tf_op jit(solution)/shard_map/ppermute | solution.py:183
  203.7 7.8 %collective-permute-start.4 = (bf16[4,48,192]{2,1,0:T(8,128)(2,1)S(1)}, bf16[4,48,192]{2,1,0:T(8,128)(2,1)S(1)}, u32[]{:S(2)}, u32[]{:S(2)}) collective-permute-start(bf16[4,48,192]{2,1,0:T(8,128)(2,1)S(1)} %copy.32), channel_id=1, source_target_pairs={{0,128},{64,192},{128,0},{192,64},{1,129},{65,193},{129,1},{193,65... | collective-permute-start | bytes 221192 | tf_op jit(solution)/shard_map/ppermute | solution.py:183
  206.7 4.8 %collective-permute-start.5 = (bf16[4,48,192]{2,1,0:T(8,128)(2,1)S(1)}, bf16[4,48,192]{2,1,0:T(8,128)(2,1)S(1)}, u32[]{:S(2)}, u32[]{:S(2)}) collective-permute-start(bf16[4,48,192]{2,1,0:T(8,128)(2,1)S(1)} %copy.31), channel_id=1, source_target_pairs={{0,192},{64,0},{128,64},{192,128},{1,193},{65,1},{129,65},{193,129... | collective-permute-start | bytes 221192 | tf_op jit(solution)/shard_map/ppermute | solution.py:183
  212.2 6.4 %collective-permute-start.6 = (bf16[4,48,192]{2,1,0:T(8,128)(2,1)S(1)}, bf16[4,48,192]{2,1,0:T(8,128)(2,1)S(1)}, u32[]{:S(2)}, u32[]{:S(2)}) collective-permute-start(bf16[4,48,192]{2,1,0:T(8,128)(2,1)S(1)} %get-tuple-element.31), channel_id=1, source_target_pairs={{0,64},{64,128},{128,192},{192,0},{1,65},{65,129},{129,193},{193,1... | collective-permute-start | bytes 221192 | tf_op jit(solution)/shard_map/ppermute | solution.py:183
  213.6 6.2 %collective-permute-start.7 = (bf16[4,48,192]{2,1,0:T(8,128)(2,1)S(1)}, bf16[4,48,192]{2,1,0:T(8,128)(2,1)S(1)}, u32[]{:S(2)}, u32[]{:S(2)}) collective-permute-start(bf16[4,48,192]{2,1,0:T(8,128)(2,1)S(1)} %get-tuple-element.31), channel_id=1, source_target_pairs={{0,128},{64,192},{128,0},{192,64},{1,129},{65,193},{129,1},{193,65... | collective-permute-start | bytes 221192 | tf_op jit(solution)/shard_map/ppermute | solution.py:183
  216.1 4.6 %collective-permute-start.8 = (bf16[4,48,192]{2,1,0:T(8,128)(2,1)S(1)}, bf16[4,48,192]{2,1,0:T(8,128)(2,1)S(1)}, u32[]{:S(2)}, u32[]{:S(2)}) collective-permute-start(bf16[4,48,192]{2,1,0:T(8,128)(2,1)S(1)} %get-tuple-element.31), channel_id=1, source_target_pairs={{0,192},{64,0},{128,64},{192,128},{1,193},{65,1},{129,65},{193,129... | collective-permute-start | bytes 221192 | tf_op jit(solution)/shard_map/ppermute | solution.py:183
  218.7 2.1 copy-start.8
  219.8 1.0 copy-start.10
  220.8 0.6 copy-start.12
  250.6 1.6 copy-start
  257.2 10.5 %collective-permute-start.10 = (bf16[3,64,256]{2,1,0:T(8,128)(2,1)}, bf16[3,64,256]{2,1,0:T(8,128)(2,1)S(1)}, u32[]{:S(2)}, u32[]{:S(2)}) collective-permute-start(bf16[3,64,256]{2,1,0:T(8,128)(2,1)} %get-tuple-element.26), channel_id=1, source_target_pairs={{0,128},{64,192},{128,0},{192,64},{1,129},{65,193},{129,1},{193,65... | collective-permute-start | bytes 294920 | tf_op jit(solution)/shard_map/ppermute | solution.py:183
  260.4 7.2 %collective-permute-start.11 = (bf16[3,64,256]{2,1,0:T(8,128)(2,1)}, bf16[3,64,256]{2,1,0:T(8,128)(2,1)S(1)}, u32[]{:S(2)}, u32[]{:S(2)}) collective-permute-start(bf16[3,64,256]{2,1,0:T(8,128)(2,1)} %get-tuple-element.27), channel_id=1, source_target_pairs={{0,192},{64,0},{128,64},{192,128},{1,193},{65,1},{129,65},{193,129... | collective-permute-start | bytes 294920 | tf_op jit(solution)/shard_map/ppermute | solution.py:183
  261.5 6.2 %copy-start.6 = (f32[3,64,256]{2,1,0:T(8,128)S(1)}, f32[3,64,256]{2,1,0:T(8,128)}, u32[]{:S(2)}) copy-start(f32[3,64,256]{2,1,0:T(8,128)} %get-tuple-element.24) | copy-start | bytes 589828
  261.5 6.2 %collective-permute-start.9 = (bf16[3,64,256]{2,1,0:T(8,128)(2,1)}, bf16[3,64,256]{2,1,0:T(8,128)(2,1)S(1)}, u32[]{:S(2)}, u32[]{:S(2)}) collective-permute-start(bf16[3,64,256]{2,1,0:T(8,128)(2,1)} %get-tuple-element.25), channel_id=1, source_target_pairs={{0,64},{64,128},{128,192},{192,0},{1,65},{65,129},{129,193},{193,1... | collective-permute-start | bytes 294920 | tf_op jit(solution)/shard_map/ppermute | solution.py:183
  268.4 6.1 %collective-permute-start.12 = (bf16[3,64,256]{2,1,0:T(8,128)(2,1)S(1)}, bf16[3,64,256]{2,1,0:T(8,128)(2,1)S(1)}, u32[]{:S(2)}, u32[]{:S(2)}) collective-permute-start(bf16[3,64,256]{2,1,0:T(8,128)(2,1)S(1)} %get-tuple-element.29), channel_id=1, source_target_pairs={{0,64},{64,128},{128,192},{192,0},{1,65},{65,129},{129,193},{193,1... | collective-permute-start | bytes 294920 | tf_op jit(solution)/shard_map/ppermute | solution.py:183
  269.1 6.7 %collective-permute-start.13 = (bf16[3,64,256]{2,1,0:T(8,128)(2,1)S(1)}, bf16[3,64,256]{2,1,0:T(8,128)(2,1)S(1)}, u32[]{:S(2)}, u32[]{:S(2)}) collective-permute-start(bf16[3,64,256]{2,1,0:T(8,128)(2,1)S(1)} %get-tuple-element.29), channel_id=1, source_target_pairs={{0,128},{64,192},{128,0},{192,64},{1,129},{65,193},{129,1},{193,65... | collective-permute-start | bytes 294920 | tf_op jit(solution)/shard_map/ppermute | solution.py:183
  272.2 4.6 %collective-permute-start.14 = (bf16[3,64,256]{2,1,0:T(8,128)(2,1)S(1)}, bf16[3,64,256]{2,1,0:T(8,128)(2,1)S(1)}, u32[]{:S(2)}, u32[]{:S(2)}) collective-permute-start(bf16[3,64,256]{2,1,0:T(8,128)(2,1)S(1)} %get-tuple-element.29), channel_id=1, source_target_pairs={{0,192},{64,0},{128,64},{192,128},{1,193},{65,1},{129,65},{193,129... | collective-permute-start | bytes 294920 | tf_op jit(solution)/shard_map/ppermute | solution.py:183
  274.5 2.3 copy-start.7
  275.8 1.0 copy-start.9
  276.8 0.6 copy-start.11

commit v3 on v2

--- a/solution.py
+++ b/solution.py
@@ -7,7 +7,7 @@
 
 X, Z, C, Y = 4, 8, 2, 4
 F32, BF16 = jnp.float32, jnp.bfloat16
-VMEM_BYTES = 56 * 2**20
+VMEM_BYTES = 62 * 2**20
 
 
 def spot(x, z, c):
@@ -42,22 +42,47 @@
     return pl.CostEstimate(flops=flops, bytes_accessed=moved_bytes, transcendentals=0)
 
 
-def gate_kernel(gates_ref, grad_ref, out_ref):
-    width = gates_ref.shape[-1]
-    for n in range(gates_ref.shape[0]):
-        p = gates_ref[n, 0].astype(F32) * grad_ref[n, 0].astype(F32)
-        out_ref[:, :, 0, :, n * width : (n + 1) * width] = p.astype(BF16)
+def gate_kernel(gates, grad_out, out, gates_held, grad_held, out_held, in_sems, out_sems):
+    count, A3 = gates.shape[:2]
+    width = gates.shape[-1]
+    reads, writes = [], []
+    for a in range(A3):
+        for n in range(count):
+            pair = [
+                pltpu.make_async_copy(gates.at[n, a], gates_held.at[n, a], in_sems.at[a, n, 0]),
+                pltpu.make_async_copy(grad_out.at[n, a], grad_held.at[n, a], in_sems.at[a, n, 1]),
+            ]
+            for copy in pair:
+                copy.start()
+            reads.append(pair)
+    for a in range(A3):
+        for n in range(count):
+            for copy in reads[a * count + n]:
+                copy.wait()
+            p = gates_held[n, a].astype(F32) * grad_held[n, a].astype(F32)
+            out_held[:, :, a, :, n * width : (n + 1) * width] = p.astype(BF16)
+        writes.append(pltpu.make_async_copy(out_held.at[:, :, a], out.at[:, :, a], out_sems.at[a]))
+        writes[-1].start()
+    for copy in writes:
+        copy.wait()
 
 
 def gate(gates, grad_out):
     count, A3, _, _, C8, width = gates.shape
-    spec = pl.BlockSpec((count, 1, X, Z, C8, width), lambda a: (0, a, 0, 0, 0, 0))
+    shape = (X, Z, A3, C8, count * width)
+    anywhere = pl.BlockSpec(memory_space=pl.ANY)
     return pl.pallas_call(
         gate_kernel,
-        grid=(A3,),
-        in_specs=[spec, spec],
-        out_specs=pl.BlockSpec((X, Z, 1, C8, count * width), lambda a: (0, 0, a, 0, 0)),
-        out_shape=jax.ShapeDtypeStruct((X, Z, A3, C8, count * width), BF16),
+        in_specs=[anywhere] * 2,
+        out_specs=anywhere,
+        out_shape=jax.ShapeDtypeStruct(shape, BF16),
+        scratch_shapes=[
+            pltpu.VMEM(gates.shape, BF16),
+            pltpu.VMEM(gates.shape, BF16),
+            pltpu.VMEM(shape, BF16),
+            pltpu.SemaphoreType.DMA((A3, count, 2)),
+            pltpu.SemaphoreType.DMA((A3,)),
+        ],
         compiler_params=params(),
         cost_estimate=cost(gates.size, 6 * gates.size),
         name="gate",
@@ -98,7 +123,7 @@
 
 def inner_product(own_m, other_m, own, other):
     rows, width = own.shape
-    tile = 256
+    tile = 512
     whole = pl.BlockSpec((rows, rows), lambda i: (0, 0))
     part = pl.BlockSpec((rows, tile), lambda i: (0, i))
     return pl.pallas_call(
@@ -113,9 +138,7 @@
     )(own_m, other_m, own, other)
 
 
-def first_kernel(y_ref, inputs_ref, inner_ref, own_ref, *refs):
-    outs, held = refs[: Y - 1], refs[Y - 1]
-    y = y_ref[0]
+def first_kernel(inputs_ref, inner_ref, own_ref, sent_ref):
     rows, width = inputs_ref.shape[2:]
     total = None
     for n in range(inputs_ref.shape[0]):
@@ -124,34 +147,27 @@
             inputs_ref[n, 0], inner, (((1,), (1,)), ((), ())), preferred_element_type=F32
         )
         total = product if total is None else total + product
-    held[...] = total.reshape(held.shape)
-    own_ref[0] = held[y]
-    for k, out in enumerate(outs):
-        out[0] = held[lax.rem(y + k + 1, Y)].astype(BF16)
-
-
-def first_gradient(y, inputs, inner):
+    own_ref[0] = total
+    sent_ref[0] = total.astype(BF16)
+
+
+def first_gradient(inputs, inner):
     count, A3, B, width = inputs.shape
-    rows = B // Y
-    index = lambda a, y: (a, 0, 0)
-    part = (A3, rows, B)
+    index = lambda a: (a, 0, 0)
+    shape = (A3, B, B)
     return pl.pallas_call(
         first_kernel,
-        grid_spec=pltpu.PrefetchScalarGridSpec(
-            num_scalar_prefetch=1,
-            grid=(A3,),
-            in_specs=[
-                pl.BlockSpec((count, 1, B, width), lambda a, y: (0, a, 0, 0)),
-                pl.BlockSpec((X * Z, 1, B // (X * Z), count * width), lambda a, y: (0, a, 0, 0)),
-            ],
-            out_specs=[pl.BlockSpec((1, rows, B), index)] * Y,
-            scratch_shapes=[pltpu.VMEM((Y, rows, B), F32)],
-        ),
-        out_shape=[jax.ShapeDtypeStruct(part, F32)] + [jax.ShapeDtypeStruct(part, BF16)] * (Y - 1),
+        grid=(A3,),
+        in_specs=[
+            pl.BlockSpec((count, 1, B, width), lambda a: (0, a, 0, 0)),
+            pl.BlockSpec((X * Z, 1, B // (X * Z), count * width), lambda a: (0, a, 0, 0)),
+        ],
+        out_specs=[pl.BlockSpec((1, B, B), index)] * 2,
+        out_shape=[jax.ShapeDtypeStruct(shape, F32), jax.ShapeDtypeStruct(shape, BF16)],
         compiler_params=params(),
         cost_estimate=cost(2 * inputs.size * B, 4 * inputs.size),
         name="first",
-    )(y, inputs, inner)
+    )(inputs, inner)
 
 
 def result_kernel(weights_ref, inner_ref, out_ref):
@@ -183,33 +199,10 @@
     return lax.ppermute(array, "dp", [(i, (i + k) % Y) for i in range(Y)])
 
 
-def place_kernel(y_ref, *refs):
-    parts, out = refs[:Y], refs[Y]
-    y = y_ref[0]
-    rows = parts[0].shape[1]
-    for k in range(Y):
-        at = pl.multiple_of(lax.rem(y + Y - k, Y) * rows, rows)
-        out[:, pl.ds(at, rows), :] = parts[k][...].astype(F32)
-
-
-def dp_sum(y, own, sent):
-    got = [dp_hop(piece, k + 1) for k, piece in enumerate(sent)]
-    for piece in got:
-        own = own + piece.astype(F32)
-    small = own.astype(BF16)
-    parts = [own] + [dp_hop(small, k) for k in range(1, Y)]
-    scalar = pl.BlockSpec(memory_space=pltpu.SMEM)
-    whole = pl.BlockSpec(memory_space=pltpu.VMEM)
-    a, b, c = own.shape
-    return pl.pallas_call(
-        place_kernel,
-        in_specs=[scalar] + [whole] * Y,
-        out_specs=whole,
-        out_shape=jax.ShapeDtypeStruct((a, b * Y, c), F32),
-        compiler_params=params(),
-        cost_estimate=cost(own.size, 6 * own.size),
-        name="place",
-    )(y, *parts)
+def dp_sum(own, sent):
+    for k in range(1, Y):
+        own = own + dp_hop(sent, k).astype(F32)
+    return own
 
 
 def shards(values, gates, grad_out, first_blocks, second_blocks):
@@ -222,7 +215,6 @@
     lanes = count * width
     here = lax.axis_index("seq").astype(jnp.int32)
     core = here % C
-    ys = lax.axis_index("dp").astype(jnp.int32).reshape(1)
 
     gates = gates.reshape(count, A3, X, Z, C8, width)
     grad_out = grad_out.reshape(count, A3, X, Z, C8, width)
@@ -281,18 +273,13 @@
         core == 0, jnp.concatenate([mine, other], 2), jnp.concatenate([other, mine], 2)
     )
     pair = pair.reshape(C4, A, A)
-    parts = [
-        lax.dynamic_slice_in_dim(pair, (ys[0] + k) % Y * (A // Y), A // Y, 1) for k in range(Y)
-    ]
-    grad_second = dp_sum(ys, parts[0], [part.astype(BF16) for part in parts[1:]])
-
+    grad_second = dp_sum(pair, pair.astype(BF16))
     inner, grad_second = lax.optimization_barrier((inner, grad_second))
 
-    own, *sent = first_gradient(ys, inputs, inner)
+    own, sent = first_gradient(inputs, inner)
     grad_values = result(first_blocks, inner, inputs.shape).reshape(count, rows, width)
     own, grad_values = lax.optimization_barrier((own, grad_values))
-    grad_first = dp_sum(ys, own, sent)
-    return grad_values, grad_first, grad_second
+    return grad_values, dp_sum(own, sent), grad_second
 
 
 def solution(mesh):

time: 282 us -> 280 us (level)
  waiting for transfers between devices: 160 us -> 188 us
  local copies, waits for them, and re-layouts: 14.6 us -> 3.36 us
  starting transfers between devices: 45.2 us -> 37 us
  Pallas kernels: 35.5 us -> 28.8 us
    ppermute x12 -> x6, waiting for transfers between devices: 11.2 us -> 25.8 us  [dp_hop(): return lax.ppermute(array, 'dp', [(i, (i + k) % Y) for i in range(Y)])]
    all_to_all x3, waiting for transfers between devices: 144 us -> 156 us  [everywhere(): lax.all_to_all(array, 'seq', 0, 0, axis_index_groups=CHIPS, tiled=True)]
    ppermute x12 -> x6, starting transfers between devices: 20.4 us -> 11.7 us  [dp_hop(): return lax.ppermute(array, 'dp', [(i, (i + k) % Y) for i in range(Y)])]
    pallas_call x4 -> x2, Pallas kernels: 14.3 us -> 9.45 us  [the longest x1 5.08 us: first_gradient(): pl.pallas_call(first_kernel, grid=(A3,), in_specs=[pl.BlockSpec((count, 1...]
  transfers between devices with their start and end apart: 18 -> 12, of which waited for: 13 -> 9; matrix products, arithmetic and copies ran while one was open for 12% -> 8% of each run, Pallas kernels for 8% -> 7%
where the time goes in v3:
time: 280 us; the launch traced here: 279 us
  waiting for transfers between devices  188 us (67%)
  starting transfers between devices  37 us (13%)
  Pallas kernels  28.8 us (10%)
  matrix products  17.4 us (6%)
  local copies, waits for them, and re-layouts  3.36 us (1%)
  other arithmetic  3.3 us (1%)
    all_to_all x3, waiting for transfers between devices, everywhere(): lax.all_to_all(array, 'seq', 0, 0, axis_index_groups=CHIPS, tiled=True)  156 us
    ppermute x6, waiting for transfers between devices, dp_hop(): return lax.ppermute(array, 'dp', [(i, (i + k) % Y) for i in range(Y)])  25.8 us
    all_to_all x3, starting transfers between devices, everywhere(): lax.all_to_all(array, 'seq', 0, 0, axis_index_groups=CHIPS, tiled=True)  24.5 us
    ppermute x6, starting transfers between devices, dp_hop(): return lax.ppermute(array, 'dp', [(i, (i + k) % Y) for i in range(Y)])  11.7 us
    dot_general x2, matrix products, shards(): lax.dot_general(cols_u, cols_g[r], (((1,), (1,)), ((), ())), preferred_el...  11 us
    pallas_call x1, Pallas kernels, inner_product(): pl.pallas_call(inner_kernel, grid=(width // tile,), in_specs=[whole, whol...  8.91 us
    ppermute x3, waiting for transfers between devices, hop(): return lax.ppermute(array, 'seq', moved(dx, dz, dc))  6.53 us
  transfers between devices with their start and end apart: 12, of which 9 were waited for; matrix products, arithmetic and copies ran while one was open for 8% of the time, Pallas kernels for 7%

profile of v3, /device:TPU:96, one launch (start us, length us, event | category | flops | bytes accessed | tf_op | source)
XLA Modules:
  0.0 278.9 jit_solution(17717193905555070273)
XLA Ops:
  0.6 4.4 %gate.1 = bf16[4,8,3,8,2048]{4,3,2,1,0:T(8,128)(2,1)} custom-call(bf16[2,3,4,8,8,1024]{5,4,3,2,1,0:T(8,128)(2,1)} %bitcast.51, bf16[2,3,4,8,8,1024]{5,4,3,2,1,0:T(8,128)(2,1)} %bitcast.52), custom_call_target="tpu_custom_call" | custom-call | flops 1572864 | bytes 9437184 | tf_op jit(solution)/shard_map/gate/pallas_call | solution.py:74
  5.0 0.0 copy-start
  5.0 10.5 %all-to-all-start = ((bf16[32,24,2048]{2,1,0:T(8,128)(2,1)}), bf16[32,24,2048]{2,1,0:T(8,128)(2,1)}, u32[]{:S(2)}, u32[]{:S(2)}) async-start(bf16[32,24,2048]{2,1,0:T(8,128)(2,1)} %bitcast.48), calls=%async_computation | async-start | bytes 6291456 | tf_op jit(solution)/shard_map/all_to_all | solution.py:34
  15.5 0.0 copy-done
  15.5 0.9 copy.14
  16.4 5.2 %mix.1 = bf16[4,8,3,8,2048]{4,3,2,1,0:T(8,128)(2,1)} custom-call(bf16[3,256,256]{2,1,0:T(8,128)(2,1)} %bitcast.54, bf16[2,3,256,1024]{3,2,1,0:T(8,128)(2,1)} %bitcast.45), custom_call_target="tpu_custom_call" | custom-call | flops 805306368 | bytes 6291456 | tf_op jit(solution)/shard_map/mix/pallas_call | solution.py:103
  21.6 67.5 %all-to-all-done = bf16[32,24,2048]{2,1,0:T(8,128)(2,1)} async-done(((bf16[32,24,2048]{2,1,0:T(8,128)(2,1)}), bf16[32,24,2048]{2,1,0:T(8,128)(2,1)}, u32[]{:S(2)}, u32[]{:S(2)}) %all-to-all-start) | async-done | bytes 3145760 | tf_op jit(solution)/shard_map/all_to_all | solution.py:34
  89.2 0.0 copy-start.2
  89.2 7.0 %all-to-all-start.1 = ((bf16[32,24,2048]{2,1,0:T(8,128)(2,1)}), bf16[32,24,2048]{2,1,0:T(8,128)(2,1)}, u32[]{:S(2)}, u32[]{:S(2)}) async-start(bf16[32,24,2048]{2,1,0:T(8,128)(2,1)} %bitcast.47), calls=%async_computation.1 | async-start | bytes 6291456 | tf_op jit(solution)/shard_map/all_to_all | solution.py:34
  96.2 0.1 collective-permute-start.1
  96.3 0.0 copy-done.2
  96.3 0.3 copy.13
  96.7 0.1 dynamic-slice_bitcast_fusion.2
  96.8 0.6 collective-permute-start
  97.4 4.8 %collective-permute-done = bf16[4,32,3,192]{3,0,2,1:T(4,128)(2,1)S(1)} collective-permute-done((bf16[4,32,3,192]{3,0,2,1:T(4,128)(2,1)S(1)}, bf16[4,32,3,192]{3,0,2,1:T(4,128)(2,1)S(1)}, u32[]{:S(2)}, u32[]{:S(2)}) %collective-permute-start) | collective-permute-done | bytes 147488 | tf_op jit(solution)/shard_map/ppermute | solution.py:30
  102.2 0.3 maximum_select_fusion.1
  102.5 0.2 select_n.118
  102.8 1.5 select_convert_fusion.other_m_ref
  104.3 1.5 select_convert_fusion.1.own_m_ref
  105.9 0.0 collective-permute-done.1.other_ref
  105.9 8.9 %inner.1 = bf16[768,2048]{1,0:T(8,128)(2,1)} custom-call(bf16[768,768]{1,0:T(8,128)(2,1)} %select_convert_fusion.1.own_m_ref, bf16[768,768]{1,0:T(8,128)(2,1)} %select_convert_fusion.other_m_ref, bf16[768,2048]{1,0:T(8,128)(2,1)} %bitcast.11.own_ref, bf16[768,2048]{1,0:T(8,128)(2,1)} %collective-permute-done.1.other_ref), custom_call_target="tpu_custom_call" | custom-call | flops 4831838208 | bytes 9437184 | tf_op jit(solution)/shard_map/inner/pallas_call | solution.py:129
  114.8 54.9 %all-to-all-done.1 = bf16[32,24,2048]{2,1,0:T(8,128)(2,1)} async-done(((bf16[32,24,2048]{2,1,0:T(8,128)(2,1)}), bf16[32,24,2048]{2,1,0:T(8,128)(2,1)}, u32[]{:S(2)}, u32[]{:S(2)}) %all-to-all-start.1) | async-done | bytes 3145760 | tf_op jit(solution)/shard_map/all_to_all | solution.py:34
  169.6 7.1 %all-to-all-start.2 = ((bf16[32,24,2048]{2,1,0:T(8,128)(2,1)}), bf16[32,24,2048]{2,1,0:T(8,128)(2,1)}, u32[]{:S(2)}, u32[]{:S(2)}) async-start(bf16[32,24,2048]{2,1,0:T(8,128)(2,1)} %bitcast.49), calls=%async_computation.2 | async-start | bytes 6291456 | tf_op jit(solution)/shard_map/all_to_all | solution.py:34
  176.7 5.5 %fusion.58 = f32[768,768]{1,0:T(8,128)S(1)} fusion(bf16[768,2048]{1,0:T(8,128)(2,1)} %bitcast.14, bf16[768,2048]{1,0:T(8,128)(2,1)} %collective-permute-done.1.other_ref), kind=kOutput, calls=%fused_computation.72 | convolution fusion | flops 2415919104 | bytes 8650752 | tf_op jit(solution)/shard_map/dot_general | solution.py:258
  182.2 1.7 fusion
  183.9 5.5 %fusion.57 = f32[768,768]{1,0:T(8,128)S(1)} fusion(bf16[768,2048]{1,0:T(8,128)(2,1)} %bitcast.14, bf16[768,2048]{1,0:T(8,128)(2,1)} %bitcast.11.own_ref), kind=kOutput, calls=%fused_computation.71 | convolution fusion | flops 2415919104 | bytes 8650752 | tf_op jit(solution)/shard_map/dot_general | solution.py:258
  189.4 1.7 fusion.4
  191.1 0.3 copy.15
  191.3 0.2 reshape.74
  191.6 0.1 constant_dynamic-slice_fusion
  191.7 0.1 collective-permute-start.2
  191.8 1.7 collective-permute-done.2
  193.5 0.2 maximum_select_fusion
  193.7 0.1 copy.16
  193.8 0.2 bitcast_convert_fusion
  194.0 1.6 collective-permute-start.3
  195.7 2.9 %collective-permute-start.4 = (bf16[4,192,192]{2,0,1:T(4,128)(2,1)S(1)}, bf16[4,192,192]{2,0,1:T(4,128)(2,1)S(1)}, u32[]{:S(2)}, u32[]{:S(2)}) collective-permute-start(bf16[4,192,192]{2,0,1:T(4,128)(2,1)S(1)} %bitcast_convert_fusion), channel_id=1, source_target_pairs={{0,128},{64,192},{128,0},{192,64},{1,129},{65,193},{129,1},{193,65... | collective-permute-start | bytes 884744 | tf_op jit(solution)/shard_map/ppermute | solution.py:199
  198.6 1.3 collective-permute-start.5
  199.9 6.6 %collective-permute-done.3 = bf16[4,192,192]{2,0,1:T(4,128)(2,1)S(1)} collective-permute-done((bf16[4,192,192]{2,0,1:T(4,128)(2,1)S(1)}, bf16[4,192,192]{2,0,1:T(4,128)(2,1)S(1)}, u32[]{:S(2)}, u32[]{:S(2)}) %collective-permute-start.3) | collective-permute-done | bytes 294944 | tf_op jit(solution)/shard_map/ppermute | solution.py:199
  206.5 9.6 %collective-permute-done.4 = bf16[4,192,192]{2,0,1:T(4,128)(2,1)S(1)} collective-permute-done((bf16[4,192,192]{2,0,1:T(4,128)(2,1)S(1)}, bf16[4,192,192]{2,0,1:T(4,128)(2,1)S(1)}, u32[]{:S(2)}, u32[]{:S(2)}) %collective-permute-start.4) | collective-permute-done | bytes 294944 | tf_op jit(solution)/shard_map/ppermute | solution.py:199
  216.1 0.0 collective-permute-done.5
  216.1 0.5 fusion.14
  216.6 33.4 %all-to-all-done.2 = bf16[32,24,2048]{2,1,0:T(8,128)(2,1)} async-done(((bf16[32,24,2048]{2,1,0:T(8,128)(2,1)}), bf16[32,24,2048]{2,1,0:T(8,128)(2,1)}, u32[]{:S(2)}, u32[]{:S(2)}) %all-to-all-start.2) | async-done | bytes 3145760 | tf_op jit(solution)/shard_map/all_to_all | solution.py:34
  250.0 5.1 %first.1 = (f32[3,256,256]{2,1,0:T(8,128)}, bf16[3,256,256]{2,1,0:T(8,128)(2,1)}) custom-call(bf16[2,3,256,1024]{3,2,1,0:T(8,128)(2,1)} %bitcast.46, bf16[32,3,8,2048]{3,2,1,0:T(8,128)(2,1)} %bitcast.16.inner_ref), custom_call_target="tpu_custom_call" | custom-call | flops 805306368 | bytes 6291456 | tf_op jit(solution)/shard_map/first/pallas_call | solution.py:158
  255.1 0.0 copy-start.1
  255.1 1.6 collective-permute-start.6
  256.7 2.9 %collective-permute-start.7 = (bf16[3,256,256]{2,1,0:T(8,128)(2,1)}, bf16[3,256,256]{2,1,0:T(8,128)(2,1)}, u32[]{:S(2)}, u32[]{:S(2)}) collective-permute-start(bf16[3,256,256]{2,1,0:T(8,128)(2,1)} %get-tuple-element.23), channel_id=1, source_target_pairs={{0,128},{64,192},{128,0},{192,64},{1,129},{65,193},{129,1},{193,65... | collective-permute-start | bytes 1179656 | tf_op jit(solution)/shard_map/ppermute | solution.py:199
  259.6 1.3 collective-permute-start.8
  260.9 5.2 %result.1 = bf16[2,3,256,1024]{3,2,1,0:T(8,128)(2,1)} custom-call(bf16[3,256,256]{2,1,0:T(8,128)(2,1)} %weights_ref, bf16[32,3,8,2048]{3,2,1,0:T(8,128)(2,1)} %bitcast.16.inner_ref), custom_call_target="tpu_custom_call" | custom-call | flops 805306368 | bytes 6291456 | tf_op jit(solution)/shard_map/result/pallas_call | solution.py:183
  266.1 1.0 copy.17
  267.1 0.3 collective-permute-done.6
  267.4 9.3 %collective-permute-done.7 = bf16[3,256,256]{2,1,0:T(8,128)(2,1)} collective-permute-done((bf16[3,256,256]{2,1,0:T(8,128)(2,1)}, bf16[3,256,256]{2,1,0:T(8,128)(2,1)}, u32[]{:S(2)}, u32[]{:S(2)}) %collective-permute-start.7) | collective-permute-done | bytes 393248 | tf_op jit(solution)/shard_map/ppermute | solution.py:199
  276.8 0.0 collective-permute-done.8
  276.8 0.0 copy-done.1
  276.8 2.2 convert_add_fusion
  (3 shorter events, 0.0 us)
Async XLA Ops:
  5.0 10.5 %copy-start = (bf16[3,256,256]{2,1,0:T(8,128)(2,1)S(1)}, bf16[3,256,256]{2,1,0:T(8,128)(2,1)}, u32[]{:S(2)}) copy-start(bf16[3,256,256]{2,1,0:T(8,128)(2,1)} %weights_ref) | copy-start | bytes 1179652
  5.0 84.2 %all-to-all-start = ((bf16[32,24,2048]{2,1,0:T(8,128)(2,1)}), bf16[32,24,2048]{2,1,0:T(8,128)(2,1)}, u32[]{:S(2)}, u32[]{:S(2)}) async-start(bf16[32,24,2048]{2,1,0:T(8,128)(2,1)} %bitcast.48), calls=%async_computation | async-start | bytes 6291456 | tf_op jit(solution)/shard_map/all_to_all | solution.py:34
  89.2 7.1 %copy-start.2 = (bf16[4,192,192]{2,1,0:T(8,128)(2,1)S(1)}, bf16[4,192,192]{2,1,0:T(8,128)(2,1)}, u32[]{:S(2)}) copy-start(bf16[4,192,192]{2,1,0:T(8,128)(2,1)} %param.9) | copy-start | bytes 884740
  89.2 80.4 %all-to-all-start.1 = ((bf16[32,24,2048]{2,1,0:T(8,128)(2,1)}), bf16[32,24,2048]{2,1,0:T(8,128)(2,1)}, u32[]{:S(2)}, u32[]{:S(2)}) async-start(bf16[32,24,2048]{2,1,0:T(8,128)(2,1)} %bitcast.47), calls=%async_computation.1 | async-start | bytes 6291456 | tf_op jit(solution)/shard_map/all_to_all | solution.py:34
  96.2 9.7 %collective-permute-start.1 = (bf16[768,2048]{1,0:T(8,128)(2,1)}, bf16[768,2048]{1,0:T(8,128)(2,1)}, u32[]{:S(2)}, u32[]{:S(2)}) collective-permute-start(bf16[768,2048]{1,0:T(8,128)(2,1)} %bitcast.11.own_ref), channel_id=1, source_target_pairs={{0,1},{1,0},{2,3},{3,2},{4,5},{5,4},{6,7},{7,6},{8,9},{9,8},{10,11... | collective-permute-start | bytes 9437192 | tf_op jit(solution)/shard_map/ppermute | solution.py:30
  96.8 5.4 %collective-permute-start = (bf16[4,32,3,192]{3,0,2,1:T(4,128)(2,1)S(1)}, bf16[4,32,3,192]{3,0,2,1:T(4,128)(2,1)S(1)}, u32[]{:S(2)}, u32[]{:S(2)}) collective-permute-start(bf16[4,32,3,192]{3,0,2,1:T(4,128)(2,1)S(1)} %get-tuple-element.31), channel_id=1, source_target_pairs={{0,1},{1,0},{2,3},{3,2},{4,5},{5,4},{6,7},{7,6},{8,9},{9,8},{10,11... | collective-permute-start | bytes 442376 | tf_op jit(solution)/shard_map/ppermute | solution.py:30
  169.6 80.4 %all-to-all-start.2 = ((bf16[32,24,2048]{2,1,0:T(8,128)(2,1)}), bf16[32,24,2048]{2,1,0:T(8,128)(2,1)}, u32[]{:S(2)}, u32[]{:S(2)}) async-start(bf16[32,24,2048]{2,1,0:T(8,128)(2,1)} %bitcast.49), calls=%async_computation.2 | async-start | bytes 6291456 | tf_op jit(solution)/shard_map/all_to_all | solution.py:34
  191.7 1.8 collective-permute-start.2
  194.0 12.5 %collective-permute-start.3 = (bf16[4,192,192]{2,0,1:T(4,128)(2,1)S(1)}, bf16[4,192,192]{2,0,1:T(4,128)(2,1)S(1)}, u32[]{:S(2)}, u32[]{:S(2)}) collective-permute-start(bf16[4,192,192]{2,0,1:T(4,128)(2,1)S(1)} %bitcast_convert_fusion), channel_id=1, source_target_pairs={{0,64},{64,128},{128,192},{192,0},{1,65},{65,129},{129,193},{193,1... | collective-permute-start | bytes 884744 | tf_op jit(solution)/shard_map/ppermute | solution.py:199
  195.7 20.5 %collective-permute-start.4 = (bf16[4,192,192]{2,0,1:T(4,128)(2,1)S(1)}, bf16[4,192,192]{2,0,1:T(4,128)(2,1)S(1)}, u32[]{:S(2)}, u32[]{:S(2)}) collective-permute-start(bf16[4,192,192]{2,0,1:T(4,128)(2,1)S(1)} %bitcast_convert_fusion), channel_id=1, source_target_pairs={{0,128},{64,192},{128,0},{192,64},{1,129},{65,193},{129,1},{193,65... | collective-permute-start | bytes 884744 | tf_op jit(solution)/shard_map/ppermute | solution.py:199
  198.6 17.6 %collective-permute-start.5 = (bf16[4,192,192]{2,0,1:T(4,128)(2,1)S(1)}, bf16[4,192,192]{2,0,1:T(4,128)(2,1)S(1)}, u32[]{:S(2)}, u32[]{:S(2)}) collective-permute-start(bf16[4,192,192]{2,0,1:T(4,128)(2,1)S(1)} %bitcast_convert_fusion), channel_id=1, source_target_pairs={{0,192},{64,0},{128,64},{192,128},{1,193},{65,1},{129,65},{193,129... | collective-permute-start | bytes 884744 | tf_op jit(solution)/shard_map/ppermute | solution.py:199
  255.1 21.7 %copy-start.1 = (f32[3,256,256]{2,1,0:T(8,128)S(1)}, f32[3,256,256]{2,1,0:T(8,128)}, u32[]{:S(2)}) copy-start(f32[3,256,256]{2,1,0:T(8,128)} %get-tuple-element.22) | copy-start | bytes 2359300
  255.1 12.4 %collective-permute-start.6 = (bf16[3,256,256]{2,1,0:T(8,128)(2,1)}, bf16[3,256,256]{2,1,0:T(8,128)(2,1)S(1)}, u32[]{:S(2)}, u32[]{:S(2)}) collective-permute-start(bf16[3,256,256]{2,1,0:T(8,128)(2,1)} %get-tuple-element.23), channel_id=1, source_target_pairs={{0,64},{64,128},{128,192},{192,0},{1,65},{65,129},{129,193},{193,1... | collective-permute-start | bytes 1179656 | tf_op jit(solution)/shard_map/ppermute | solution.py:199
  256.7 20.1 %collective-permute-start.7 = (bf16[3,256,256]{2,1,0:T(8,128)(2,1)}, bf16[3,256,256]{2,1,0:T(8,128)(2,1)}, u32[]{:S(2)}, u32[]{:S(2)}) collective-permute-start(bf16[3,256,256]{2,1,0:T(8,128)(2,1)} %get-tuple-element.23), channel_id=1, source_target_pairs={{0,128},{64,192},{128,0},{192,64},{1,129},{65,193},{129,1},{193,65... | collective-permute-start | bytes 1179656 | tf_op jit(solution)/shard_map/ppermute | solution.py:199
  259.6 17.2 %collective-permute-start.8 = (bf16[3,256,256]{2,1,0:T(8,128)(2,1)}, bf16[3,256,256]{2,1,0:T(8,128)(2,1)}, u32[]{:S(2)}, u32[]{:S(2)}) collective-permute-start(bf16[3,256,256]{2,1,0:T(8,128)(2,1)} %get-tuple-element.23), channel_id=1, source_target_pairs={{0,192},{64,0},{128,64},{192,128},{1,193},{65,1},{129,65},{193,129... | collective-permute-start | bytes 1179656 | tf_op jit(solution)/shard_map/ppermute | solution.py:199

commit v4 on v3

--- a/solution.py
+++ b/solution.py
@@ -277,9 +277,12 @@
     inner, grad_second = lax.optimization_barrier((inner, grad_second))
 
     own, sent = first_gradient(inputs, inner)
+    got = [dp_hop(sent, k) for k in range(1, Y)]
     grad_values = result(first_blocks, inner, inputs.shape).reshape(count, rows, width)
-    own, grad_values = lax.optimization_barrier((own, grad_values))
-    return grad_values, dp_sum(own, sent), grad_second
+    got, grad_values = lax.optimization_barrier((got, grad_values))
+    for piece in got:
+        own = own + piece.astype(F32)
+    return grad_values, own, grad_second
 
 
 def solution(mesh):

time: 280 us -> 278 us (level)
  no operation moved by 1% of the time
where the time goes in v4:
time: 278 us
  waiting for transfers between devices  188 us (68%)
  starting transfers between devices  37 us (13%)
  Pallas kernels  28.9 us (10%)
  matrix products  17.4 us (6%)
  local copies, waits for them, and re-layouts  3.36 us (1%)
    all_to_all x3, waiting for transfers between devices, everywhere(): lax.all_to_all(array, 'seq', 0, 0, axis_index_groups=CHIPS, tiled=True)  156 us
    ppermute x6, waiting for transfers between devices, dp_hop(): return lax.ppermute(array, 'dp', [(i, (i + k) % Y) for i in range(Y)])  25.7 us
    all_to_all x3, starting transfers between devices, everywhere(): lax.all_to_all(array, 'seq', 0, 0, axis_index_groups=CHIPS, tiled=True)  24.5 us
    ppermute x6, starting transfers between devices, dp_hop(): return lax.ppermute(array, 'dp', [(i, (i + k) % Y) for i in range(Y)])  11.7 us
    dot_general x2, matrix products, shards(): lax.dot_general(cols_u, cols_g[r], (((1,), (1,)), ((), ())), preferred_el...  11 us
    pallas_call x1, Pallas kernels, inner_product(): pl.pallas_call(inner_kernel, grid=(width // tile,), in_specs=[whole, whol...  8.91 us
    ppermute x3, waiting for transfers between devices, hop(): return lax.ppermute(array, 'seq', moved(dx, dz, dc))  6.53 us
  transfers between devices with their start and end apart: 12, of which 9 were waited for; matrix products, arithmetic and copies ran while one was open for 8% of the time, Pallas kernels for 7%

profile of v4, /device:TPU:96, one launch (start us, length us, event | category | flops | bytes accessed | tf_op | source)
XLA Modules:
  0.0 277.7 jit_solution(10615769353395565589)
XLA Ops:
  0.6 4.4 %gate.1 = bf16[4,8,3,8,2048]{4,3,2,1,0:T(8,128)(2,1)} custom-call(bf16[2,3,4,8,8,1024]{5,4,3,2,1,0:T(8,128)(2,1)} %bitcast.51, bf16[2,3,4,8,8,1024]{5,4,3,2,1,0:T(8,128)(2,1)} %bitcast.52), custom_call_target="tpu_custom_call" | custom-call | flops 1572864 | bytes 9437184 | tf_op jit(solution)/shard_map/gate/pallas_call | solution.py:74
  5.0 0.0 copy-start
  5.0 10.5 %all-to-all-start = ((bf16[32,24,2048]{2,1,0:T(8,128)(2,1)}), bf16[32,24,2048]{2,1,0:T(8,128)(2,1)}, u32[]{:S(2)}, u32[]{:S(2)}) async-start(bf16[32,24,2048]{2,1,0:T(8,128)(2,1)} %bitcast.48), calls=%async_computation | async-start | bytes 6291456 | tf_op jit(solution)/shard_map/all_to_all | solution.py:34
  15.5 0.0 copy-done
  15.5 0.9 copy.14
  16.4 5.2 %mix.1 = bf16[4,8,3,8,2048]{4,3,2,1,0:T(8,128)(2,1)} custom-call(bf16[3,256,256]{2,1,0:T(8,128)(2,1)} %bitcast.54, bf16[2,3,256,1024]{3,2,1,0:T(8,128)(2,1)} %bitcast.45), custom_call_target="tpu_custom_call" | custom-call | flops 805306368 | bytes 6291456 | tf_op jit(solution)/shard_map/mix/pallas_call | solution.py:103
  21.7 67.5 %all-to-all-done = bf16[32,24,2048]{2,1,0:T(8,128)(2,1)} async-done(((bf16[32,24,2048]{2,1,0:T(8,128)(2,1)}), bf16[32,24,2048]{2,1,0:T(8,128)(2,1)}, u32[]{:S(2)}, u32[]{:S(2)}) %all-to-all-start) | async-done | bytes 3145760 | tf_op jit(solution)/shard_map/all_to_all | solution.py:34
  89.2 0.0 copy-start.2
  89.2 7.0 %all-to-all-start.1 = ((bf16[32,24,2048]{2,1,0:T(8,128)(2,1)}), bf16[32,24,2048]{2,1,0:T(8,128)(2,1)}, u32[]{:S(2)}, u32[]{:S(2)}) async-start(bf16[32,24,2048]{2,1,0:T(8,128)(2,1)} %bitcast.47), calls=%async_computation.1 | async-start | bytes 6291456 | tf_op jit(solution)/shard_map/all_to_all | solution.py:34
  96.2 0.1 collective-permute-start.1
  96.3 0.0 copy-done.2
  96.3 0.3 copy.13
  96.7 0.1 dynamic-slice_bitcast_fusion.2
  96.8 0.6 collective-permute-start
  97.4 4.8 %collective-permute-done = bf16[4,32,3,192]{3,0,2,1:T(4,128)(2,1)S(1)} collective-permute-done((bf16[4,32,3,192]{3,0,2,1:T(4,128)(2,1)S(1)}, bf16[4,32,3,192]{3,0,2,1:T(4,128)(2,1)S(1)}, u32[]{:S(2)}, u32[]{:S(2)}) %collective-permute-start) | collective-permute-done | bytes 147488 | tf_op jit(solution)/shard_map/ppermute | solution.py:30
  102.2 0.3 maximum_select_fusion.1
  102.5 0.2 select_n.118
  102.8 1.5 select_convert_fusion.other_m_ref
  104.3 1.5 select_convert_fusion.1.own_m_ref
  105.9 0.0 collective-permute-done.1.other_ref
  105.9 8.9 %inner.1 = bf16[768,2048]{1,0:T(8,128)(2,1)} custom-call(bf16[768,768]{1,0:T(8,128)(2,1)} %select_convert_fusion.1.own_m_ref, bf16[768,768]{1,0:T(8,128)(2,1)} %select_convert_fusion.other_m_ref, bf16[768,2048]{1,0:T(8,128)(2,1)} %bitcast.11.own_ref, bf16[768,2048]{1,0:T(8,128)(2,1)} %collective-permute-done.1.other_ref), custom_call_target="tpu_custom_call" | custom-call | flops 4831838208 | bytes 9437184 | tf_op jit(solution)/shard_map/inner/pallas_call | solution.py:129
  114.8 54.9 %all-to-all-done.1 = bf16[32,24,2048]{2,1,0:T(8,128)(2,1)} async-done(((bf16[32,24,2048]{2,1,0:T(8,128)(2,1)}), bf16[32,24,2048]{2,1,0:T(8,128)(2,1)}, u32[]{:S(2)}, u32[]{:S(2)}) %all-to-all-start.1) | async-done | bytes 3145760 | tf_op jit(solution)/shard_map/all_to_all | solution.py:34
  169.6 7.1 %all-to-all-start.2 = ((bf16[32,24,2048]{2,1,0:T(8,128)(2,1)}), bf16[32,24,2048]{2,1,0:T(8,128)(2,1)}, u32[]{:S(2)}, u32[]{:S(2)}) async-start(bf16[32,24,2048]{2,1,0:T(8,128)(2,1)} %bitcast.49), calls=%async_computation.2 | async-start | bytes 6291456 | tf_op jit(solution)/shard_map/all_to_all | solution.py:34
  176.7 5.5 %fusion.58 = f32[768,768]{1,0:T(8,128)S(1)} fusion(bf16[768,2048]{1,0:T(8,128)(2,1)} %bitcast.14, bf16[768,2048]{1,0:T(8,128)(2,1)} %collective-permute-done.1.other_ref), kind=kOutput, calls=%fused_computation.72 | convolution fusion | flops 2415919104 | bytes 8650752 | tf_op jit(solution)/shard_map/dot_general | solution.py:258
  182.2 1.7 fusion
  183.9 5.5 %fusion.57 = f32[768,768]{1,0:T(8,128)S(1)} fusion(bf16[768,2048]{1,0:T(8,128)(2,1)} %bitcast.14, bf16[768,2048]{1,0:T(8,128)(2,1)} %bitcast.11.own_ref), kind=kOutput, calls=%fused_computation.71 | convolution fusion | flops 2415919104 | bytes 8650752 | tf_op jit(solution)/shard_map/dot_general | solution.py:258
  189.4 1.7 fusion.4
  191.1 0.3 copy.15
  191.3 0.2 reshape.74
  191.6 0.1 constant_dynamic-slice_fusion
  191.7 0.1 collective-permute-start.2
  191.8 1.7 collective-permute-done.2
  193.5 0.2 maximum_select_fusion
  193.7 0.1 copy.16
  193.8 0.2 bitcast_convert_fusion
  194.0 1.6 collective-permute-start.3
  195.7 2.9 %collective-permute-start.4 = (bf16[4,192,192]{2,0,1:T(4,128)(2,1)S(1)}, bf16[4,192,192]{2,0,1:T(4,128)(2,1)S(1)}, u32[]{:S(2)}, u32[]{:S(2)}) collective-permute-start(bf16[4,192,192]{2,0,1:T(4,128)(2,1)S(1)} %bitcast_convert_fusion), channel_id=1, source_target_pairs={{0,128},{64,192},{128,0},{192,64},{1,129},{65,193},{129,1},{193,65... | collective-permute-start | bytes 884744 | tf_op jit(solution)/shard_map/ppermute | solution.py:199
  198.6 1.3 collective-permute-start.5
  199.9 6.6 %collective-permute-done.3 = bf16[4,192,192]{2,0,1:T(4,128)(2,1)S(1)} collective-permute-done((bf16[4,192,192]{2,0,1:T(4,128)(2,1)S(1)}, bf16[4,192,192]{2,0,1:T(4,128)(2,1)S(1)}, u32[]{:S(2)}, u32[]{:S(2)}) %collective-permute-start.3) | collective-permute-done | bytes 294944 | tf_op jit(solution)/shard_map/ppermute | solution.py:199
  206.5 9.6 %collective-permute-done.4 = bf16[4,192,192]{2,0,1:T(4,128)(2,1)S(1)} collective-permute-done((bf16[4,192,192]{2,0,1:T(4,128)(2,1)S(1)}, bf16[4,192,192]{2,0,1:T(4,128)(2,1)S(1)}, u32[]{:S(2)}, u32[]{:S(2)}) %collective-permute-start.4) | collective-permute-done | bytes 294944 | tf_op jit(solution)/shard_map/ppermute | solution.py:199
  216.1 0.0 collective-permute-done.5
  216.1 0.5 fusion.14
  216.6 33.4 %all-to-all-done.2 = bf16[32,24,2048]{2,1,0:T(8,128)(2,1)} async-done(((bf16[32,24,2048]{2,1,0:T(8,128)(2,1)}), bf16[32,24,2048]{2,1,0:T(8,128)(2,1)}, u32[]{:S(2)}, u32[]{:S(2)}) %all-to-all-start.2) | async-done | bytes 3145760 | tf_op jit(solution)/shard_map/all_to_all | solution.py:34
  250.0 5.1 %first.1 = (f32[3,256,256]{2,1,0:T(8,128)}, bf16[3,256,256]{2,1,0:T(8,128)(2,1)}) custom-call(bf16[2,3,256,1024]{3,2,1,0:T(8,128)(2,1)} %bitcast.46, bf16[32,3,8,2048]{3,2,1,0:T(8,128)(2,1)} %bitcast.16.inner_ref), custom_call_target="tpu_custom_call" | custom-call | flops 805306368 | bytes 6291456 | tf_op jit(solution)/shard_map/first/pallas_call | solution.py:158
  255.1 1.6 collective-permute-start.6
  256.7 2.9 %collective-permute-start.7 = (bf16[3,256,256]{2,1,0:T(8,128)(2,1)}, bf16[3,256,256]{2,1,0:T(8,128)(2,1)S(1)}, u32[]{:S(2)}, u32[]{:S(2)}) collective-permute-start(bf16[3,256,256]{2,1,0:T(8,128)(2,1)} %get-tuple-element.22), channel_id=1, source_target_pairs={{0,128},{64,192},{128,0},{192,64},{1,129},{65,193},{129,1},{193,65... | collective-permute-start | bytes 1179656 | tf_op jit(solution)/shard_map/ppermute | solution.py:199
  259.6 1.3 collective-permute-start.8
  260.9 1.0 copy.17
  261.9 0.0 copy-start.1
  261.9 5.3 %result.1 = bf16[2,3,256,1024]{3,2,1,0:T(8,128)(2,1)} custom-call(bf16[3,256,256]{2,1,0:T(8,128)(2,1)} %weights_ref, bf16[32,3,8,2048]{3,2,1,0:T(8,128)(2,1)} %bitcast.16.inner_ref), custom_call_target="tpu_custom_call" | custom-call | flops 805306368 | bytes 6291456 | tf_op jit(solution)/shard_map/result/pallas_call | solution.py:183
  267.2 0.2 collective-permute-done.6
  267.4 9.2 %collective-permute-done.7 = bf16[3,256,256]{2,1,0:T(8,128)(2,1)S(1)} collective-permute-done((bf16[3,256,256]{2,1,0:T(8,128)(2,1)}, bf16[3,256,256]{2,1,0:T(8,128)(2,1)S(1)}, u32[]{:S(2)}, u32[]{:S(2)}) %collective-permute-start.7) | collective-permute-done | bytes 393248 | tf_op jit(solution)/shard_map/ppermute | solution.py:199
  276.7 0.0 collective-permute-done.8
  276.7 0.0 copy-done.1
  276.7 1.0 convert_add_fusion
  (3 shorter events, 0.0 us)
Async XLA Ops:
  5.0 10.5 %copy-start = (bf16[3,256,256]{2,1,0:T(8,128)(2,1)S(1)}, bf16[3,256,256]{2,1,0:T(8,128)(2,1)}, u32[]{:S(2)}) copy-start(bf16[3,256,256]{2,1,0:T(8,128)(2,1)} %weights_ref) | copy-start | bytes 1179652
  5.0 84.2 %all-to-all-start = ((bf16[32,24,2048]{2,1,0:T(8,128)(2,1)}), bf16[32,24,2048]{2,1,0:T(8,128)(2,1)}, u32[]{:S(2)}, u32[]{:S(2)}) async-start(bf16[32,24,2048]{2,1,0:T(8,128)(2,1)} %bitcast.48), calls=%async_computation | async-start | bytes 6291456 | tf_op jit(solution)/shard_map/all_to_all | solution.py:34
  89.2 7.1 %copy-start.2 = (bf16[4,192,192]{2,1,0:T(8,128)(2,1)S(1)}, bf16[4,192,192]{2,1,0:T(8,128)(2,1)}, u32[]{:S(2)}) copy-start(bf16[4,192,192]{2,1,0:T(8,128)(2,1)} %param.9) | copy-start | bytes 884740
  89.2 80.4 %all-to-all-start.1 = ((bf16[32,24,2048]{2,1,0:T(8,128)(2,1)}), bf16[32,24,2048]{2,1,0:T(8,128)(2,1)}, u32[]{:S(2)}, u32[]{:S(2)}) async-start(bf16[32,24,2048]{2,1,0:T(8,128)(2,1)} %bitcast.47), calls=%async_computation.1 | async-start | bytes 6291456 | tf_op jit(solution)/shard_map/all_to_all | solution.py:34
  96.2 9.7 %collective-permute-start.1 = (bf16[768,2048]{1,0:T(8,128)(2,1)}, bf16[768,2048]{1,0:T(8,128)(2,1)}, u32[]{:S(2)}, u32[]{:S(2)}) collective-permute-start(bf16[768,2048]{1,0:T(8,128)(2,1)} %bitcast.11.own_ref), channel_id=1, source_target_pairs={{0,1},{1,0},{2,3},{3,2},{4,5},{5,4},{6,7},{7,6},{8,9},{9,8},{10,11... | collective-permute-start | bytes 9437192 | tf_op jit(solution)/shard_map/ppermute | solution.py:30
  96.8 5.4 %collective-permute-start = (bf16[4,32,3,192]{3,0,2,1:T(4,128)(2,1)S(1)}, bf16[4,32,3,192]{3,0,2,1:T(4,128)(2,1)S(1)}, u32[]{:S(2)}, u32[]{:S(2)}) collective-permute-start(bf16[4,32,3,192]{3,0,2,1:T(4,128)(2,1)S(1)} %get-tuple-element.35), channel_id=1, source_target_pairs={{0,1},{1,0},{2,3},{3,2},{4,5},{5,4},{6,7},{7,6},{8,9},{9,8},{10,11... | collective-permute-start | bytes 442376 | tf_op jit(solution)/shard_map/ppermute | solution.py:30
  169.6 80.4 %all-to-all-start.2 = ((bf16[32,24,2048]{2,1,0:T(8,128)(2,1)}), bf16[32,24,2048]{2,1,0:T(8,128)(2,1)}, u32[]{:S(2)}, u32[]{:S(2)}) async-start(bf16[32,24,2048]{2,1,0:T(8,128)(2,1)} %bitcast.49), calls=%async_computation.2 | async-start | bytes 6291456 | tf_op jit(solution)/shard_map/all_to_all | solution.py:34
  191.7 1.8 collective-permute-start.2
  194.0 12.5 %collective-permute-start.3 = (bf16[4,192,192]{2,0,1:T(4,128)(2,1)S(1)}, bf16[4,192,192]{2,0,1:T(4,128)(2,1)S(1)}, u32[]{:S(2)}, u32[]{:S(2)}) collective-permute-start(bf16[4,192,192]{2,0,1:T(4,128)(2,1)S(1)} %bitcast_convert_fusion), channel_id=1, source_target_pairs={{0,64},{64,128},{128,192},{192,0},{1,65},{65,129},{129,193},{193,1... | collective-permute-start | bytes 884744 | tf_op jit(solution)/shard_map/ppermute | solution.py:199
  195.7 20.5 %collective-permute-start.4 = (bf16[4,192,192]{2,0,1:T(4,128)(2,1)S(1)}, bf16[4,192,192]{2,0,1:T(4,128)(2,1)S(1)}, u32[]{:S(2)}, u32[]{:S(2)}) collective-permute-start(bf16[4,192,192]{2,0,1:T(4,128)(2,1)S(1)} %bitcast_convert_fusion), channel_id=1, source_target_pairs={{0,128},{64,192},{128,0},{192,64},{1,129},{65,193},{129,1},{193,65... | collective-permute-start | bytes 884744 | tf_op jit(solution)/shard_map/ppermute | solution.py:199
  198.6 17.6 %collective-permute-start.5 = (bf16[4,192,192]{2,0,1:T(4,128)(2,1)S(1)}, bf16[4,192,192]{2,0,1:T(4,128)(2,1)S(1)}, u32[]{:S(2)}, u32[]{:S(2)}) collective-permute-start(bf16[4,192,192]{2,0,1:T(4,128)(2,1)S(1)} %bitcast_convert_fusion), channel_id=1, source_target_pairs={{0,192},{64,0},{128,64},{192,128},{1,193},{65,1},{129,65},{193,129... | collective-permute-start | bytes 884744 | tf_op jit(solution)/shard_map/ppermute | solution.py:199
  255.1 12.4 %collective-permute-start.6 = (bf16[3,256,256]{2,1,0:T(8,128)(2,1)}, bf16[3,256,256]{2,1,0:T(8,128)(2,1)S(1)}, u32[]{:S(2)}, u32[]{:S(2)}) collective-permute-start(bf16[3,256,256]{2,1,0:T(8,128)(2,1)} %get-tuple-element.22), channel_id=1, source_target_pairs={{0,64},{64,128},{128,192},{192,0},{1,65},{65,129},{129,193},{193,1... | collective-permute-start | bytes 1179656 | tf_op jit(solution)/shard_map/ppermute | solution.py:199
  256.7 20.0 %collective-permute-start.7 = (bf16[3,256,256]{2,1,0:T(8,128)(2,1)}, bf16[3,256,256]{2,1,0:T(8,128)(2,1)S(1)}, u32[]{:S(2)}, u32[]{:S(2)}) collective-permute-start(bf16[3,256,256]{2,1,0:T(8,128)(2,1)} %get-tuple-element.22), channel_id=1, source_target_pairs={{0,128},{64,192},{128,0},{192,64},{1,129},{65,193},{129,1},{193,65... | collective-permute-start | bytes 1179656 | tf_op jit(solution)/shard_map/ppermute | solution.py:199
  259.6 17.1 %collective-permute-start.8 = (bf16[3,256,256]{2,1,0:T(8,128)(2,1)}, bf16[3,256,256]{2,1,0:T(8,128)(2,1)S(1)}, u32[]{:S(2)}, u32[]{:S(2)}) collective-permute-start(bf16[3,256,256]{2,1,0:T(8,128)(2,1)} %get-tuple-element.22), channel_id=1, source_target_pairs={{0,192},{64,0},{128,64},{192,128},{1,193},{65,1},{129,65},{193,129... | collective-permute-start | bytes 1179656 | tf_op jit(solution)/shard_map/ppermute | solution.py:199
  261.9 14.7 %copy-start.1 = (f32[3,256,256]{2,1,0:T(8,128)S(1)}, f32[3,256,256]{2,1,0:T(8,128)}, u32[]{:S(2)}) copy-start(f32[3,256,256]{2,1,0:T(8,128)} %get-tuple-element.24) | copy-start | bytes 2359300

commit v5 on v4

--- a/solution.py
+++ b/solution.py
@@ -138,7 +138,7 @@
     )(own_m, other_m, own, other)
 
 
-def first_kernel(inputs_ref, inner_ref, own_ref, sent_ref):
+def first_kernel(inputs_ref, inner_ref, own_ref, left_ref, right_ref):
     rows, width = inputs_ref.shape[2:]
     total = None
     for n in range(inputs_ref.shape[0]):
@@ -148,13 +148,15 @@
         )
         total = product if total is None else total + product
     own_ref[0] = total
-    sent_ref[0] = total.astype(BF16)
+    half = total.shape[1] // 2
+    left_ref[0] = total[:, :half].astype(BF16)
+    right_ref[0] = total[:, half:].astype(BF16)
 
 
 def first_gradient(inputs, inner):
     count, A3, B, width = inputs.shape
     index = lambda a: (a, 0, 0)
-    shape = (A3, B, B)
+    half = jax.ShapeDtypeStruct((A3, B, B // 2), BF16)
     return pl.pallas_call(
         first_kernel,
         grid=(A3,),
@@ -162,8 +164,8 @@
             pl.BlockSpec((count, 1, B, width), lambda a: (0, a, 0, 0)),
             pl.BlockSpec((X * Z, 1, B // (X * Z), count * width), lambda a: (0, a, 0, 0)),
         ],
-        out_specs=[pl.BlockSpec((1, B, B), index)] * 2,
-        out_shape=[jax.ShapeDtypeStruct(shape, F32), jax.ShapeDtypeStruct(shape, BF16)],
+        out_specs=[pl.BlockSpec((1, B, B), index)] + [pl.BlockSpec((1, B, B // 2), index)] * 2,
+        out_shape=[jax.ShapeDtypeStruct((A3, B, B), F32), half, half],
         compiler_params=params(),
         cost_estimate=cost(2 * inputs.size * B, 4 * inputs.size),
         name="first",
@@ -276,10 +278,17 @@
     grad_second = dp_sum(pair, pair.astype(BF16))
     inner, grad_second = lax.optimization_barrier((inner, grad_second))
 
-    own, sent = first_gradient(inputs, inner)
-    got = [dp_hop(sent, k) for k in range(1, Y)]
+    own, left, right = first_gradient(inputs, inner)
+    left_below, right_above = dp_hop(left, 1), dp_hop(right, Y - 1)
+    right_below, left_above = dp_hop(right, 1), dp_hop(left, Y - 1)
+    halves = [
+        (left_below, right_below),
+        (left_above, right_above),
+        (dp_hop(left_below, 1), dp_hop(right_above, Y - 1)),
+    ]
     grad_values = result(first_blocks, inner, inputs.shape).reshape(count, rows, width)
-    got, grad_values = lax.optimization_barrier((got, grad_values))
+    halves, grad_values = lax.optimization_barrier((halves, grad_values))
+    got = [jnp.concatenate(pair, 2) for pair in halves]
     for piece in got:
         own = own + piece.astype(F32)
     return grad_values, own, grad_second

time: 278 us -> 276 us (level)
  waiting for transfers between devices: 188 us -> 181 us
  starting transfers between devices: 37 us -> 40.9 us
    ppermute x6 -> x9, waiting for transfers between devices: 25.7 us -> 18.9 us  [dp_hop(): return lax.ppermute(array, 'dp', [(i, (i + k) % Y) for i in range(Y)])]
    ppermute x6 -> x9, starting transfers between devices: 11.7 us -> 15.6 us  [dp_hop(): return lax.ppermute(array, 'dp', [(i, (i + k) % Y) for i in range(Y)])]
  transfers between devices with their start and end apart: 12 -> 15, of which waited for: 9 -> 8; matrix products, arithmetic and copies ran while one was open for 8% -> 8% of each run, Pallas kernels for 7% -> 7%
where the time goes in v5:
time: 276 us; the launch traced here: 275 us
  waiting for transfers between devices  181 us (66%)
  starting transfers between devices  40.9 us (15%)
  Pallas kernels  28.9 us (10%)
  matrix products  17.4 us (6%)
  local copies, waits for them, and re-layouts  3.36 us (1%)
    all_to_all x3, waiting for transfers between devices, everywhere(): lax.all_to_all(array, 'seq', 0, 0, axis_index_groups=CHIPS, tiled=True)  156 us
    all_to_all x3, starting transfers between devices, everywhere(): lax.all_to_all(array, 'seq', 0, 0, axis_index_groups=CHIPS, tiled=True)  24.5 us
    ppermute x9, waiting for transfers between devices, dp_hop(): return lax.ppermute(array, 'dp', [(i, (i + k) % Y) for i in range(Y)])  18.9 us
    ppermute x9, starting transfers between devices, dp_hop(): return lax.ppermute(array, 'dp', [(i, (i + k) % Y) for i in range(Y)])  15.6 us
    dot_general x2, matrix products, shards(): lax.dot_general(cols_u, cols_g[r], (((1,), (1,)), ((), ())), preferred_el...  11 us
    pallas_call x1, Pallas kernels, inner_product(): pl.pallas_call(inner_kernel, grid=(width // tile,), in_specs=[whole, whol...  8.91 us
    ppermute x3, waiting for transfers between devices, hop(): return lax.ppermute(array, 'seq', moved(dx, dz, dc))  6.53 us
  transfers between devices with their start and end apart: 15, of which 8 were waited for; matrix products, arithmetic and copies ran while one was open for 8% of the time, Pallas kernels for 7%

profile of v5, /device:TPU:96, one launch (start us, length us, event | category | flops | bytes accessed | tf_op | source)
XLA Modules:
  0.0 274.9 jit_solution(16626486489043197884)
XLA Ops:
  0.6 4.4 %gate.1 = bf16[4,8,3,8,2048]{4,3,2,1,0:T(8,128)(2,1)} custom-call(bf16[2,3,4,8,8,1024]{5,4,3,2,1,0:T(8,128)(2,1)} %bitcast.51, bf16[2,3,4,8,8,1024]{5,4,3,2,1,0:T(8,128)(2,1)} %bitcast.52), custom_call_target="tpu_custom_call" | custom-call | flops 1572864 | bytes 9437184 | tf_op jit(solution)/shard_map/gate/pallas_call | solution.py:74
  5.0 0.0 copy-start
  5.0 10.5 %all-to-all-start = ((bf16[32,24,2048]{2,1,0:T(8,128)(2,1)}), bf16[32,24,2048]{2,1,0:T(8,128)(2,1)}, u32[]{:S(2)}, u32[]{:S(2)}) async-start(bf16[32,24,2048]{2,1,0:T(8,128)(2,1)} %bitcast.48), calls=%async_computation | async-start | bytes 6291456 | tf_op jit(solution)/shard_map/all_to_all | solution.py:34
  15.5 0.0 copy-done
  15.5 0.9 copy.14
  16.4 5.3 %mix.1 = bf16[4,8,3,8,2048]{4,3,2,1,0:T(8,128)(2,1)} custom-call(bf16[3,256,256]{2,1,0:T(8,128)(2,1)} %bitcast.54, bf16[2,3,256,1024]{3,2,1,0:T(8,128)(2,1)} %bitcast.45), custom_call_target="tpu_custom_call" | custom-call | flops 805306368 | bytes 6291456 | tf_op jit(solution)/shard_map/mix/pallas_call | solution.py:103
  21.7 67.5 %all-to-all-done = bf16[32,24,2048]{2,1,0:T(8,128)(2,1)} async-done(((bf16[32,24,2048]{2,1,0:T(8,128)(2,1)}), bf16[32,24,2048]{2,1,0:T(8,128)(2,1)}, u32[]{:S(2)}, u32[]{:S(2)}) %all-to-all-start) | async-done | bytes 3145760 | tf_op jit(solution)/shard_map/all_to_all | solution.py:34
  89.2 0.0 copy-start.2
  89.2 7.0 %all-to-all-start.1 = ((bf16[32,24,2048]{2,1,0:T(8,128)(2,1)}), bf16[32,24,2048]{2,1,0:T(8,128)(2,1)}, u32[]{:S(2)}, u32[]{:S(2)}) async-start(bf16[32,24,2048]{2,1,0:T(8,128)(2,1)} %bitcast.47), calls=%async_computation.1 | async-start | bytes 6291456 | tf_op jit(solution)/shard_map/all_to_all | solution.py:34
  96.2 0.1 collective-permute-start.1
  96.3 0.0 copy-done.2
  96.3 0.3 copy.13
  96.7 0.1 dynamic-slice_bitcast_fusion.2
  96.8 0.6 collective-permute-start
  97.4 4.8 %collective-permute-done = bf16[4,32,3,192]{3,0,2,1:T(4,128)(2,1)S(1)} collective-permute-done((bf16[4,32,3,192]{3,0,2,1:T(4,128)(2,1)S(1)}, bf16[4,32,3,192]{3,0,2,1:T(4,128)(2,1)S(1)}, u32[]{:S(2)}, u32[]{:S(2)}) %collective-permute-start) | collective-permute-done | bytes 147488 | tf_op jit(solution)/shard_map/ppermute | solution.py:30
  102.2 0.3 maximum_select_fusion.1
  102.5 0.2 select_n.118
  102.8 1.5 select_convert_fusion.other_m_ref
  104.3 1.6 select_convert_fusion.1.own_m_ref
  105.9 0.0 collective-permute-done.1.other_ref
  105.9 8.9 %inner.1 = bf16[768,2048]{1,0:T(8,128)(2,1)} custom-call(bf16[768,768]{1,0:T(8,128)(2,1)} %select_convert_fusion.1.own_m_ref, bf16[768,768]{1,0:T(8,128)(2,1)} %select_convert_fusion.other_m_ref, bf16[768,2048]{1,0:T(8,128)(2,1)} %bitcast.11.own_ref, bf16[768,2048]{1,0:T(8,128)(2,1)} %collective-permute-done.1.other_ref), custom_call_target="tpu_custom_call" | custom-call | flops 4831838208 | bytes 9437184 | tf_op jit(solution)/shard_map/inner/pallas_call | solution.py:129
  114.8 54.8 %all-to-all-done.1 = bf16[32,24,2048]{2,1,0:T(8,128)(2,1)} async-done(((bf16[32,24,2048]{2,1,0:T(8,128)(2,1)}), bf16[32,24,2048]{2,1,0:T(8,128)(2,1)}, u32[]{:S(2)}, u32[]{:S(2)}) %all-to-all-start.1) | async-done | bytes 3145760 | tf_op jit(solution)/shard_map/all_to_all | solution.py:34
  169.6 7.1 %all-to-all-start.2 = ((bf16[32,24,2048]{2,1,0:T(8,128)(2,1)}), bf16[32,24,2048]{2,1,0:T(8,128)(2,1)}, u32[]{:S(2)}, u32[]{:S(2)}) async-start(bf16[32,24,2048]{2,1,0:T(8,128)(2,1)} %bitcast.49), calls=%async_computation.2 | async-start | bytes 6291456 | tf_op jit(solution)/shard_map/all_to_all | solution.py:34
  176.7 5.5 %fusion.58 = f32[768,768]{1,0:T(8,128)S(1)} fusion(bf16[768,2048]{1,0:T(8,128)(2,1)} %bitcast.14, bf16[768,2048]{1,0:T(8,128)(2,1)} %collective-permute-done.1.other_ref), kind=kOutput, calls=%fused_computation.72 | convolution fusion | flops 2415919104 | bytes 8650752 | tf_op jit(solution)/shard_map/dot_general | solution.py:260
  182.2 1.7 fusion
  183.9 5.5 %fusion.57 = f32[768,768]{1,0:T(8,128)S(1)} fusion(bf16[768,2048]{1,0:T(8,128)(2,1)} %bitcast.14, bf16[768,2048]{1,0:T(8,128)(2,1)} %bitcast.11.own_ref), kind=kOutput, calls=%fused_computation.71 | convolution fusion | flops 2415919104 | bytes 8650752 | tf_op jit(solution)/shard_map/dot_general | solution.py:260
  189.4 1.7 fusion.4
  191.1 0.3 copy.15
  191.3 0.2 reshape.74
  191.6 0.1 constant_dynamic-slice_fusion
  191.7 0.1 collective-permute-start.2
  191.8 1.7 collective-permute-done.2
  193.5 0.2 maximum_select_fusion
  193.7 0.1 copy.16
  193.8 0.2 bitcast_convert_fusion
  194.0 1.7 collective-permute-start.3
  195.7 2.9 %collective-permute-start.4 = (bf16[4,192,192]{2,0,1:T(4,128)(2,1)S(1)}, bf16[4,192,192]{2,0,1:T(4,128)(2,1)S(1)}, u32[]{:S(2)}, u32[]{:S(2)}) collective-permute-start(bf16[4,192,192]{2,0,1:T(4,128)(2,1)S(1)} %bitcast_convert_fusion), channel_id=1, source_target_pairs={{0,128},{64,192},{128,0},{192,64},{1,129},{65,193},{129,1},{193,65... | collective-permute-start | bytes 884744 | tf_op jit(solution)/shard_map/ppermute | solution.py:201
  198.6 1.3 collective-permute-start.5
  199.9 6.6 %collective-permute-done.3 = bf16[4,192,192]{2,0,1:T(4,128)(2,1)S(1)} collective-permute-done((bf16[4,192,192]{2,0,1:T(4,128)(2,1)S(1)}, bf16[4,192,192]{2,0,1:T(4,128)(2,1)S(1)}, u32[]{:S(2)}, u32[]{:S(2)}) %collective-permute-start.3) | collective-permute-done | bytes 294944 | tf_op jit(solution)/shard_map/ppermute | solution.py:201
  206.5 9.6 %collective-permute-done.4 = bf16[4,192,192]{2,0,1:T(4,128)(2,1)S(1)} collective-permute-done((bf16[4,192,192]{2,0,1:T(4,128)(2,1)S(1)}, bf16[4,192,192]{2,0,1:T(4,128)(2,1)S(1)}, u32[]{:S(2)}, u32[]{:S(2)}) %collective-permute-start.4) | collective-permute-done | bytes 294944 | tf_op jit(solution)/shard_map/ppermute | solution.py:201
  216.1 0.0 collective-permute-done.5
  216.1 0.5 fusion.14
  216.6 33.4 %all-to-all-done.2 = bf16[32,24,2048]{2,1,0:T(8,128)(2,1)} async-done(((bf16[32,24,2048]{2,1,0:T(8,128)(2,1)}), bf16[32,24,2048]{2,1,0:T(8,128)(2,1)}, u32[]{:S(2)}, u32[]{:S(2)}) %all-to-all-start.2) | async-done | bytes 3145760 | tf_op jit(solution)/shard_map/all_to_all | solution.py:34
  250.0 5.1 %first.1 = (f32[3,256,256]{2,1,0:T(8,128)}, bf16[3,256,128]{2,1,0:T(8,128)(2,1)}, bf16[3,256,128]{2,1,0:T(8,128)(2,1)}) custom-call(bf16[2,3,256,1024]{3,2,1,0:T(8,128)(2,1)} %bitcast.46, bf16[32,3,8,2048]{3,2,1,0:T(8,128)(2,1)} %bitcast.16.inner_ref), custom_call_target="tpu_custom_call" | custom-call | flops 805306368 | bytes 6291456 | tf_op jit(solution)/shard_map/first/pallas_call | solution.py:160
  255.1 1.6 collective-permute-start.6
  256.7 1.7 collective-permute-start.9
  258.3 0.4 collective-permute-start.7
  258.7 2.9 %collective-permute-start.8 = (bf16[3,256,128]{2,1,0:T(8,128)(2,1)}, bf16[3,256,128]{2,1,0:T(8,128)(2,1)S(1)}, u32[]{:S(2)}, u32[]{:S(2)}) collective-permute-start(bf16[3,256,128]{2,1,0:T(8,128)(2,1)} %get-tuple-element.26), channel_id=1, source_target_pairs={{0,192},{64,0},{128,64},{192,128},{1,193},{65,1},{129,65},{193,129... | collective-permute-start | bytes 589832 | tf_op jit(solution)/shard_map/ppermute | solution.py:201
  261.6 2.7 collective-permute-done.6
  264.3 0.4 collective-permute-start.10
  264.7 0.0 collective-permute-done.9
  264.7 2.8 %collective-permute-start.11 = (bf16[3,256,128]{2,1,0:T(8,128)(2,1)S(1)}, bf16[3,256,128]{2,1,0:T(8,128)(2,1)S(1)}, u32[]{:S(2)}, u32[]{:S(2)}) collective-permute-start(bf16[3,256,128]{2,1,0:T(8,128)(2,1)S(1)} %collective-permute-done.9), channel_id=1, source_target_pairs={{0,192},{64,0},{128,64},{192,128},{1,193},{65,1},{129,65},{193,129... | collective-permute-start | bytes 589832 | tf_op jit(solution)/shard_map/ppermute | solution.py:201
  267.5 1.0 copy.17
  268.5 0.0 copy-start.1
  268.5 5.3 %result.1 = bf16[2,3,256,1024]{3,2,1,0:T(8,128)(2,1)} custom-call(bf16[3,256,256]{2,1,0:T(8,128)(2,1)} %weights_ref, bf16[32,3,8,2048]{3,2,1,0:T(8,128)(2,1)} %bitcast.16.inner_ref), custom_call_target="tpu_custom_call" | custom-call | flops 805306368 | bytes 6291456 | tf_op jit(solution)/shard_map/result/pallas_call | solution.py:185
  273.8 0.0 collective-permute-done.7
  273.8 0.0 collective-permute-done.8
  273.8 0.0 collective-permute-done.10
  273.8 0.0 collective-permute-done.11
  273.8 0.0 copy-done.1
  273.8 1.1 convert_add_fusion
  (3 shorter events, 0.0 us)
Async XLA Ops:
  5.0 10.5 %copy-start = (bf16[3,256,256]{2,1,0:T(8,128)(2,1)S(1)}, bf16[3,256,256]{2,1,0:T(8,128)(2,1)}, u32[]{:S(2)}) copy-start(bf16[3,256,256]{2,1,0:T(8,128)(2,1)} %weights_ref) | copy-start | bytes 1179652
  5.0 84.2 %all-to-all-start = ((bf16[32,24,2048]{2,1,0:T(8,128)(2,1)}), bf16[32,24,2048]{2,1,0:T(8,128)(2,1)}, u32[]{:S(2)}, u32[]{:S(2)}) async-start(bf16[32,24,2048]{2,1,0:T(8,128)(2,1)} %bitcast.48), calls=%async_computation | async-start | bytes 6291456 | tf_op jit(solution)/shard_map/all_to_all | solution.py:34
  89.2 7.1 %copy-start.2 = (bf16[4,192,192]{2,1,0:T(8,128)(2,1)S(1)}, bf16[4,192,192]{2,1,0:T(8,128)(2,1)}, u32[]{:S(2)}) copy-start(bf16[4,192,192]{2,1,0:T(8,128)(2,1)} %param.9) | copy-start | bytes 884740
  89.2 80.4 %all-to-all-start.1 = ((bf16[32,24,2048]{2,1,0:T(8,128)(2,1)}), bf16[32,24,2048]{2,1,0:T(8,128)(2,1)}, u32[]{:S(2)}, u32[]{:S(2)}) async-start(bf16[32,24,2048]{2,1,0:T(8,128)(2,1)} %bitcast.47), calls=%async_computation.1 | async-start | bytes 6291456 | tf_op jit(solution)/shard_map/all_to_all | solution.py:34
  96.2 9.7 %collective-permute-start.1 = (bf16[768,2048]{1,0:T(8,128)(2,1)}, bf16[768,2048]{1,0:T(8,128)(2,1)}, u32[]{:S(2)}, u32[]{:S(2)}) collective-permute-start(bf16[768,2048]{1,0:T(8,128)(2,1)} %bitcast.11.own_ref), channel_id=1, source_target_pairs={{0,1},{1,0},{2,3},{3,2},{4,5},{5,4},{6,7},{7,6},{8,9},{9,8},{10,11... | collective-permute-start | bytes 9437192 | tf_op jit(solution)/shard_map/ppermute | solution.py:30
  96.8 5.4 %collective-permute-start = (bf16[4,32,3,192]{3,0,2,1:T(4,128)(2,1)S(1)}, bf16[4,32,3,192]{3,0,2,1:T(4,128)(2,1)S(1)}, u32[]{:S(2)}, u32[]{:S(2)}) collective-permute-start(bf16[4,32,3,192]{3,0,2,1:T(4,128)(2,1)S(1)} %get-tuple-element.43), channel_id=1, source_target_pairs={{0,1},{1,0},{2,3},{3,2},{4,5},{5,4},{6,7},{7,6},{8,9},{9,8},{10,11... | collective-permute-start | bytes 442376 | tf_op jit(solution)/shard_map/ppermute | solution.py:30
  169.6 80.4 %all-to-all-start.2 = ((bf16[32,24,2048]{2,1,0:T(8,128)(2,1)}), bf16[32,24,2048]{2,1,0:T(8,128)(2,1)}, u32[]{:S(2)}, u32[]{:S(2)}) async-start(bf16[32,24,2048]{2,1,0:T(8,128)(2,1)} %bitcast.49), calls=%async_computation.2 | async-start | bytes 6291456 | tf_op jit(solution)/shard_map/all_to_all | solution.py:34
  191.7 1.8 collective-permute-start.2
  194.0 12.5 %collective-permute-start.3 = (bf16[4,192,192]{2,0,1:T(4,128)(2,1)S(1)}, bf16[4,192,192]{2,0,1:T(4,128)(2,1)S(1)}, u32[]{:S(2)}, u32[]{:S(2)}) collective-permute-start(bf16[4,192,192]{2,0,1:T(4,128)(2,1)S(1)} %bitcast_convert_fusion), channel_id=1, source_target_pairs={{0,64},{64,128},{128,192},{192,0},{1,65},{65,129},{129,193},{193,1... | collective-permute-start | bytes 884744 | tf_op jit(solution)/shard_map/ppermute | solution.py:201
  195.7 20.4 %collective-permute-start.4 = (bf16[4,192,192]{2,0,1:T(4,128)(2,1)S(1)}, bf16[4,192,192]{2,0,1:T(4,128)(2,1)S(1)}, u32[]{:S(2)}, u32[]{:S(2)}) collective-permute-start(bf16[4,192,192]{2,0,1:T(4,128)(2,1)S(1)} %bitcast_convert_fusion), channel_id=1, source_target_pairs={{0,128},{64,192},{128,0},{192,64},{1,129},{65,193},{129,1},{193,65... | collective-permute-start | bytes 884744 | tf_op jit(solution)/shard_map/ppermute | solution.py:201
  198.6 17.6 %collective-permute-start.5 = (bf16[4,192,192]{2,0,1:T(4,128)(2,1)S(1)}, bf16[4,192,192]{2,0,1:T(4,128)(2,1)S(1)}, u32[]{:S(2)}, u32[]{:S(2)}) collective-permute-start(bf16[4,192,192]{2,0,1:T(4,128)(2,1)S(1)} %bitcast_convert_fusion), channel_id=1, source_target_pairs={{0,192},{64,0},{128,64},{192,128},{1,193},{65,1},{129,65},{193,129... | collective-permute-start | bytes 884744 | tf_op jit(solution)/shard_map/ppermute | solution.py:201
  255.1 9.2 %collective-permute-start.6 = (bf16[3,256,128]{2,1,0:T(8,128)(2,1)}, bf16[3,256,128]{2,1,0:T(8,128)(2,1)S(1)}, u32[]{:S(2)}, u32[]{:S(2)}) collective-permute-start(bf16[3,256,128]{2,1,0:T(8,128)(2,1)} %get-tuple-element.26), channel_id=1, source_target_pairs={{0,64},{64,128},{128,192},{192,0},{1,65},{65,129},{129,193},{193,1... | collective-permute-start | bytes 589832 | tf_op jit(solution)/shard_map/ppermute | solution.py:201
  256.7 8.1 %collective-permute-start.9 = (bf16[3,256,128]{2,1,0:T(8,128)(2,1)}, bf16[3,256,128]{2,1,0:T(8,128)(2,1)S(1)}, u32[]{:S(2)}, u32[]{:S(2)}) collective-permute-start(bf16[3,256,128]{2,1,0:T(8,128)(2,1)} %get-tuple-element.27), channel_id=1, source_target_pairs={{0,192},{64,0},{128,64},{192,128},{1,193},{65,1},{129,65},{193,129... | collective-permute-start | bytes 589832 | tf_op jit(solution)/shard_map/ppermute | solution.py:201
  258.3 15.5 %collective-permute-start.7 = (bf16[3,256,128]{2,1,0:T(8,128)(2,1)}, bf16[3,256,128]{2,1,0:T(8,128)(2,1)S(1)}, u32[]{:S(2)}, u32[]{:S(2)}) collective-permute-start(bf16[3,256,128]{2,1,0:T(8,128)(2,1)} %get-tuple-element.27), channel_id=1, source_target_pairs={{0,64},{64,128},{128,192},{192,0},{1,65},{65,129},{129,193},{193,1... | collective-permute-start | bytes 589832 | tf_op jit(solution)/shard_map/ppermute | solution.py:201
  258.7 15.1 %collective-permute-start.8 = (bf16[3,256,128]{2,1,0:T(8,128)(2,1)}, bf16[3,256,128]{2,1,0:T(8,128)(2,1)S(1)}, u32[]{:S(2)}, u32[]{:S(2)}) collective-permute-start(bf16[3,256,128]{2,1,0:T(8,128)(2,1)} %get-tuple-element.26), channel_id=1, source_target_pairs={{0,192},{64,0},{128,64},{192,128},{1,193},{65,1},{129,65},{193,129... | collective-permute-start | bytes 589832 | tf_op jit(solution)/shard_map/ppermute | solution.py:201
  264.3 9.5 %collective-permute-start.10 = (bf16[3,256,128]{2,1,0:T(8,128)(2,1)S(1)}, bf16[3,256,128]{2,1,0:T(8,128)(2,1)S(1)}, u32[]{:S(2)}, u32[]{:S(2)}) collective-permute-start(bf16[3,256,128]{2,1,0:T(8,128)(2,1)S(1)} %collective-permute-done.6), channel_id=1, source_target_pairs={{0,64},{64,128},{128,192},{192,0},{1,65},{65,129},{129,193},{193,1... | collective-permute-start | bytes 589832 | tf_op jit(solution)/shard_map/ppermute | solution.py:201
  264.7 9.1 %collective-permute-start.11 = (bf16[3,256,128]{2,1,0:T(8,128)(2,1)S(1)}, bf16[3,256,128]{2,1,0:T(8,128)(2,1)S(1)}, u32[]{:S(2)}, u32[]{:S(2)}) collective-permute-start(bf16[3,256,128]{2,1,0:T(8,128)(2,1)S(1)} %collective-permute-done.9), channel_id=1, source_target_pairs={{0,192},{64,0},{128,64},{192,128},{1,193},{65,1},{129,65},{193,129... | collective-permute-start | bytes 589832 | tf_op jit(solution)/shard_map/ppermute | solution.py:201
  268.5 5.3 %copy-start.1 = (f32[3,256,256]{2,1,0:T(8,128)S(1)}, f32[3,256,256]{2,1,0:T(8,128)}, u32[]{:S(2)}) copy-start(f32[3,256,256]{2,1,0:T(8,128)} %get-tuple-element.29) | copy-start | bytes 2359300
